TPU v7x, 256 devices: a whole 4x4x8 slice. The times are simulated.
256 devices in a mesh: row: 8 (over x_hi, y), col: 32 (over z, x_lo, core).
Axes of the slice: x: 4 (x_hi: 2, x_lo: 2; x = x_hi * 2 + x_lo), y: 4, z: 8, core: 2. Of those that a mesh axis runs over, the one named last changes fastest.
Arguments:
- object_field: float32 [2, 2048, 16384], P(None, 'row', 'col'), may hold values from -6 to 6
- probe: float32 [2, 256, 256], replicated, may hold values from -6 to 6
- measured: float32 [8, 32, 4, 256, 256], P('row', 'col'), may hold values from 0.5 to 4
- positions: int32 [8, 32, 4, 2], P('row', 'col'), may hold values from -128 to 16256, as said below
- counts: int32 [8, 32], P('row', 'col'), may hold values from 2 to 4, as said below
Outputs:
- object_new: float32 [2, 2048, 16384], P(None, 'row', 'col')
- probe_new: float32 [2, 256, 256], replicated
Inputs may be any that keep to these rules, and one draw needn't show every extreme that they name: `positions`: for the tile (r, c) every slot's patch starts at row r * 256 - 128 + a and column c * 512 - 128 + b with 0 <= a <= 256 and 0 <= b <= 512, also for slots that are not live. Slots from index counts[r, c] on hold no live pattern; some tile is full.
All inputs are finite; a program needn't handle non-finite values.
Results may differ from a plain program's by a relative error of at most 0.00088.
The roundings to bfloat16 on the way count: a program that leaves them out, or rounds other values in their place, can miss the bound.
Values sent between devices are 32-bit elements; how exact they have to be, the bound alone decides.
A program may use at most 128 MiB of HBM per device.

v0:
```python
import jax
import jax.numpy as jnp
from jax import lax
from jax.sharding import PartitionSpec as P


def extended(cells, sides, width):
    for axis, dim in sides:
        count = lax.axis_size(axis)
        ends = count - 1
        head = lax.slice_in_dim(cells, 0, width, axis=dim)
        tail = lax.slice_in_dim(cells, cells.shape[dim] - width, cells.shape[dim], axis=dim)
        cells = jnp.concatenate(
            [
                lax.ppermute(tail, axis, [(i, (i + 1) % count) for i in range(ends)]),
                cells,
                lax.ppermute(head, axis, [((i + 1) % count, i) for i in range(ends)]),
            ],
            axis=dim,
        )
    return cells


def tables(extent):
    indices = jnp.arange(extent, dtype=jnp.int32)
    products = indices[:, None] * indices[None, :] % extent
    angles = 2.0 * jnp.pi / extent * products.astype(jnp.float32)
    cosine = jnp.cos(angles) / jnp.sqrt(jnp.float32(extent))
    sine_part = jnp.sin(angles) / jnp.sqrt(jnp.float32(extent))
    forward = jnp.block([[cosine, -sine_part], [sine_part, cosine]]).astype(jnp.bfloat16)
    inverse = jnp.block([[cosine, sine_part], [-sine_part, cosine]]).astype(jnp.bfloat16)
    return (forward, inverse)


def product(blocks, table):
    batch_n, side_n, wide_n = blocks.shape
    flattened = blocks.reshape(batch_n * side_n, wide_n)
    return jnp.dot(flattened, table, preferred_element_type=jnp.float32).reshape(
        batch_n, side_n, wide_n
    )


def turn_planes(blocks, extent):
    batch_n = blocks.shape[0]
    return (
        blocks.reshape(batch_n, extent, 2, extent)
        .transpose(0, 3, 2, 1)
        .reshape(batch_n, extent, 2 * extent)
    )


def diffract(patches, probe, amplitudes, live_mask):
    extent = probe.shape[1]
    probe_re, probe_im = (probe[0], probe[1])
    patch_re, patch_im = (patches[:, 0], patches[:, 1])
    exit_wave = jnp.concatenate(
        [probe_re * patch_re - probe_im * patch_im, probe_re * patch_im + probe_im * patch_re],
        axis=-1,
    ).astype(jnp.bfloat16)
    forward, inverse = tables(extent)
    half_done = turn_planes(product(exit_wave, forward).astype(jnp.bfloat16), extent)
    spectrum = product(half_done, forward)
    spec_re, spec_im = (spectrum[..., :extent], spectrum[..., extent:])
    magnitude = jnp.sqrt(spec_re * spec_re + spec_im * spec_im + 0.25)
    factor = live_mask[:, None, None] * (1.0 - amplitudes / magnitude)
    residue = jnp.concatenate([factor * spec_re, factor * spec_im], axis=-1).astype(jnp.bfloat16)
    back_half = turn_planes(product(residue, inverse).astype(jnp.bfloat16), extent)
    update = product(back_half, inverse)
    update_re, update_im = (update[..., :extent], update[..., extent:])
    obj_terms = jnp.stack(
        [probe_re * update_re + probe_im * update_im, probe_re * update_im - probe_im * update_re],
        axis=1,
    )
    probe_terms = jnp.stack(
        [
            jnp.sum(patch_re * update_re + patch_im * update_im, axis=0),
            jnp.sum(patch_re * update_im - patch_im * update_re, axis=0),
            jnp.sum(live_mask[:, None, None] * (patch_re * patch_re + patch_im * patch_im), axis=0),
        ]
    )
    return (obj_terms, probe_terms)


def place_terms(canvas, term_set, corners):
    zero_index = jnp.zeros((), jnp.int32)

    def add_one(number, current):
        corner_at = (zero_index, corners[number, 0], corners[number, 1])
        section = lax.dynamic_slice(current, corner_at, term_set.shape[1:]) + term_set[number]
        return lax.dynamic_update_slice(current, section, corner_at)

    return lax.fori_loop(0, term_set.shape[0], add_one, canvas)


def return_rows(canvas, half_w):
    strips = jnp.concatenate([canvas[:, :half_w], canvas[:, -half_w:]], axis=1)
    framed = extended(strips, (("row", 1),), half_w)
    interior = canvas[:, half_w:-half_w]
    interior = interior.at[:, :half_w].add(framed[:, :half_w])
    return interior.at[:, -half_w:].add(framed[:, -half_w:])


def return_cols(canvas, half_w):
    strips = jnp.concatenate([canvas[:, :, :half_w], canvas[:, :, -half_w:]], axis=2)
    framed = extended(strips, (("col", 2),), half_w)
    interior = canvas[:, :, half_w:-half_w]
    interior = interior.at[:, :, :half_w].add(framed[:, :, :half_w])
    return interior.at[:, :, -half_w:].add(framed[:, :, -half_w:])


def body(object_field, probe, measured, positions, counts):
    extent = probe.shape[1]
    half_w = extent // 2
    tile_rows = object_field.shape[1]
    tile_cols = object_field.shape[2]
    patterns = measured.shape[2]
    row_at = lax.axis_index("row") * tile_rows
    col_at = lax.axis_index("col") * tile_cols
    zero_index = jnp.zeros((), jnp.int32)
    framed = extended(object_field, (("row", 1), ("col", 2)), half_w)
    anchor = jnp.stack([row_at - half_w, col_at - half_w])
    local_pos = positions[0, 0] - anchor[None, :]
    live_mask = (jnp.arange(patterns, dtype=jnp.int32) < counts[0, 0]).astype(jnp.float32)
    patches = jax.vmap(
        lambda corner: lax.dynamic_slice(
            framed, (zero_index, corner[0], corner[1]), (2, extent, extent)
        )
    )(local_pos)
    obj_terms, probe_terms = diffract(patches, probe, measured[0, 0], live_mask)
    probe_power = probe[0] * probe[0] + probe[1] * probe[1]
    lit = (live_mask[:, None, None] * probe_power[None])[:, None]
    term_set = jnp.concatenate([obj_terms, lit], axis=1)
    canvas = jnp.zeros(
        (term_set.shape[1], tile_rows + 2 * half_w, tile_cols + 2 * half_w), jnp.float32
    )
    canvas = place_terms(canvas, term_set, local_pos)
    gradients = return_cols(return_rows(canvas, half_w), half_w)
    illum = gradients[2]
    summed = lax.psum(probe_terms, ("row", "col"))
    peak_illum = lax.pmax(jnp.max(illum), ("row", "col"))
    weight = summed[2]
    probe_new = probe - summed[:2] / (0.75 * weight + 0.25 * jnp.max(weight))
    object_new = object_field - gradients[:2] / (0.75 * illum + 0.25 * peak_illum)
    return (object_new, probe_new)


def solution(mesh):
    in_specs = (
        P(None, "row", "col"),
        P(),
        P("row", "col", None, None, None),
        P("row", "col", None, None),
        P("row", "col"),
    )
    out_specs = (P(None, "row", "col"), P())
    return jax.shard_map(body, mesh=mesh, in_specs=in_specs, out_specs=out_specs, check_vma=False)
```

profile of v0, /device:TPU:1, one launch (start us, length us, event | category | flops | bytes accessed | tf_op | source)
XLA Modules:
  0.0 515.9 jit_solution(14446695244889101852)
XLA Ops:
  7.2 1.4 fusion.49
  8.6 1.3 collective-permute-start.1
  9.9 4.7 collective-permute-start
  15.4 1.0 fusion.40
  16.4 1.8 negate_convert_fusion
  18.2 4.7 collective-permute-done
  23.1 1.3 copy-done.6
  24.5 6.9 %collective-permute-start.2 = (f32[2,512,128]{2,1,0:T(8,128)S(1)}, f32[2,512,128]{2,1,0:T(8,128)S(1)}, u32[]{:S(2)}, u32[]{:S(2)}) collective-permute-start(f32[2,512,128]{2,1,0:T(8,128)S(1)} %get-tuple-element.181), channel_id=1, source_target_pairs={{0,1},{1,2},{2,3},{3,4},{4,5},{5,6},{6,7},{7,8},{8,9},{9,10},{10,1... | collective-permute-start | bytes 1572872 | tf_op jit(solution)/shard_map/ppermute | solution.py:15
  31.4 1.9 collective-permute-start.3
  33.5 0.7 slice_bitcast_fusion.1
  34.2 1.1 broadcast_multiply_fusion
  35.3 7.8 %collective-permute-done.2 = f32[2,512,128]{2,1,0:T(8,128)S(1)} collective-permute-done((f32[2,512,128]{2,1,0:T(8,128)S(1)}, f32[2,512,128]{2,1,0:T(8,128)S(1)}, u32[]{:S(2)}, u32[]{:S(2)}) %collective-permute-start.2) | collective-permute-done | bytes 524320 | tf_op jit(solution)/shard_map/ppermute | solution.py:15
  43.1 0.8 copy-done.17
  43.9 1.4 pad_maximum_fusion
  45.4 11.3 %while.19 = (s32[]{:T(128)}, f32[2,512,768]{2,1,0:T(8,128)S(1)}, s32[4,3]{1,0:T(4,128)S(1)}, f32[4,2,256,256]{3,2,0,1:T(8,128)}, s32[]{:T(128)}) while((s32[]{:T(128)}, f32[2,512,768]{2,1,0:T(8,128)S(1)}, s32[4,3]{1,0:T(4,128)S(1)}, f32[4,2,256,256]{3,2,0,1:T(8,128)}, s32[]{:T(128)}) %tuple.82), condition=%wide.while_cond.4, body=%wide.while_body.4.sunk | while | flops 2 | bytes 1049717 | solution.py:125
  46.0 2.2 bitcast_dynamic-update-slice_fusion.2
  48.2 0.6 fusion.53
  48.8 2.2 bitcast_dynamic-update-slice_fusion.2
  51.6 2.2 bitcast_dynamic-update-slice_fusion.2
  54.5 2.2 bitcast_dynamic-update-slice_fusion.2
  56.7 1.9 fusion.9
  58.6 0.7 convolution_convert_fusion.1
  59.6 2.0 copy.10
  61.6 0.7 dot_general.17
  62.3 0.7 fusion.31
  64.1 0.7 convolution_convert_fusion
  65.1 2.0 copy.11
  67.1 0.7 dot_general.20
  67.8 0.7 fusion.28
  68.5 0.9 copy-done.5
  69.4 1.6 fusion.13
  71.0 1.9 pad_maximum_fusion.1
  72.8 2.5 broadcast_in_dim.2
  75.3 61.4 %while.18 = (s32[]{:T(128)}, f32[3,512,768]{2,1,0:T(8,128)}, s32[4,2]{0,1:T(2,128)S(1)}, f32[4,3,256,256]{3,2,0,1:T(8,128)}, s32[]{:T(128)}, /*index=5*/s32[]{:T(128)}, s32[]{:T(128)}, s32[]{:T(128)}) while((s32[]{:T(128)}, f32[3,512,768]{2,1,0:T(8,128)}, s32[4,2]{0,1:T(2,128)S(1)}, f32[4,3,256,256]{3,2,0,1:T(8,128)}, s32[]{:T(128)}, ...), condition=%wide.region_1.2_spmd, body=%wide.region_0.1_spmd.sunk | while | flops 196616 | bytes 3932357 | solution.py:92
  75.3 0.6 constant_dynamic-slice_fusion.5
  79.8 1.8 bitcast_add_fusion.2
  81.6 8.9 %dynamic_update_slice.8 = f32[3,512,768]{2,1,0:T(8,128)} dynamic-update-slice(f32[3,512,768]{2,1,0:T(8,128)} %get-tuple-element.274, f32[3,256,256]{2,1,0:T(8,128)S(1)} %bitcast_add_fusion.2, s32[]{:T(128)} %constant.178.clone.1..sunk, s32[]{:T(128)S(6)} %select_n.70, s32[]{:T(128)S(6)} %select_n.71) | dynamic-update-slice | bytes 1572868 | tf_op jit(solution)/shard_map/while/body/eval_jaxpr/dynamic_update_slice | solution.py:90
  90.6 0.6 constant_dynamic-slice_fusion.5
  95.0 1.8 bitcast_add_fusion.2
  96.9 8.9 %dynamic_update_slice.8 = f32[3,512,768]{2,1,0:T(8,128)} dynamic-update-slice(f32[3,512,768]{2,1,0:T(8,128)} %get-tuple-element.274, f32[3,256,256]{2,1,0:T(8,128)S(1)} %bitcast_add_fusion.2, s32[]{:T(128)} %constant.178.clone.1..sunk, s32[]{:T(128)S(6)} %select_n.70, s32[]{:T(128)S(6)} %select_n.71) | dynamic-update-slice | bytes 1572868 | tf_op jit(solution)/shard_map/while/body/eval_jaxpr/dynamic_update_slice | solution.py:90
  105.8 0.6 constant_dynamic-slice_fusion.5
  110.2 1.8 bitcast_add_fusion.2
  112.1 9.4 %dynamic_update_slice.8 = f32[3,512,768]{2,1,0:T(8,128)} dynamic-update-slice(f32[3,512,768]{2,1,0:T(8,128)} %get-tuple-element.274, f32[3,256,256]{2,1,0:T(8,128)S(1)} %bitcast_add_fusion.2, s32[]{:T(128)} %constant.178.clone.1..sunk, s32[]{:T(128)S(6)} %select_n.70, s32[]{:T(128)S(6)} %select_n.71) | dynamic-update-slice | bytes 1572868 | tf_op jit(solution)/shard_map/while/body/eval_jaxpr/dynamic_update_slice | solution.py:90
  121.5 0.6 constant_dynamic-slice_fusion.5
  125.9 1.8 bitcast_add_fusion.2
  127.8 9.0 %dynamic_update_slice.8 = f32[3,512,768]{2,1,0:T(8,128)} dynamic-update-slice(f32[3,512,768]{2,1,0:T(8,128)} %get-tuple-element.274, f32[3,256,256]{2,1,0:T(8,128)S(1)} %bitcast_add_fusion.2, s32[]{:T(128)} %constant.178.clone.1..sunk, s32[]{:T(128)S(6)} %select_n.70, s32[]{:T(128)S(6)} %select_n.71) | dynamic-update-slice | bytes 1572868 | tf_op jit(solution)/shard_map/while/body/eval_jaxpr/dynamic_update_slice | solution.py:90
  136.7 3.5 fusion.46
  140.2 5.2 %collective-permute-start.4 = (f32[3,128,768]{2,1,0:T(8,128)}, f32[3,128,768]{2,1,0:T(8,128)}, u32[]{:S(2)}, u32[]{:S(2)}) collective-permute-start(f32[3,128,768]{2,1,0:T(8,128)} %get-tuple-element.170), channel_id=1, source_target_pairs={{0,32},{32,64},{64,96},{96,128},{128,160},{160,192},{192,224},{1,3... | collective-permute-start | bytes 3538952 | tf_op jit(solution)/shard_map/ppermute | solution.py:15
  145.4 1.4 collective-permute-start.5
  147.0 0.9 pad_maximum_fusion.2
  148.0 14.3 %collective-permute-done.4 = f32[3,128,768]{2,1,0:T(8,128)} collective-permute-done((f32[3,128,768]{2,1,0:T(8,128)}, f32[3,128,768]{2,1,0:T(8,128)}, u32[]{:S(2)}, u32[]{:S(2)}) %collective-permute-start.4) | collective-permute-done | bytes 1179680 | tf_op jit(solution)/shard_map/ppermute | solution.py:15
  162.3 1.8 add_dynamic-update-slice_fusion
  164.1 3.4 collective-permute-done.5
  167.8 11.6 %collective-permute-start.6 = (f32[3,256,128]{2,1,0:T(8,128)S(1)}, f32[3,256,128]{2,1,0:T(8,128)S(1)}, u32[]{:S(2)}, u32[]{:S(2)}) collective-permute-start(f32[3,256,128]{2,1,0:T(8,128)S(1)} %get-tuple-element.178), channel_id=1, source_target_pairs={{0,1},{1,2},{2,3},{3,4},{4,5},{5,6},{6,7},{7,8},{8,9},{9,10},{10,1... | collective-permute-start | bytes 1179656 | tf_op jit(solution)/shard_map/ppermute | solution.py:15
  179.4 234.0 %all-reduce.2.cloned.1.call-done = f32[3,256,256]{2,1,0:T(8,128)} async-done(((f32[3,256,256]{2,1,0:T(8,128)}), f32[3,256,256]{2,1,0:T(8,128)}) %all-reduce.2.cloned.1.call-update) | async-done | bytes 786448 | tf_op jit(solution)/shard_map/psum | solution.py:139
  413.4 1.6 slice_reduce_fusion.1
  415.7 4.0 collective-permute-start.7
  419.7 1.0 add_bitcast_fusion.2
  420.9 5.4 %collective-permute-done.7 = f32[3,256,128]{2,1,0:T(8,128)S(1)} collective-permute-done((f32[3,256,128]{2,1,0:T(8,128)S(1)}, f32[3,256,128]{2,1,0:T(8,128)S(1)}, u32[]{:S(2)}, u32[]{:S(2)}) %collective-permute-start.7) | collective-permute-done | bytes 393248 | tf_op jit(solution)/shard_map/ppermute | solution.py:17
  426.4 1.2 copy-done.1
  427.6 0.7 slice_reduce_fusion
  428.3 0.9 fusion.25
  429.2 77.9 %pmax.7 = f32[]{:T(128)} all-reduce(f32[]{:T(128)} %slice_reduce_fusion), channel_id=1, replica_groups=mesh['row'=8,'col'=32] {'row','col'}, use_global_device_ids=true, to_apply=%region_3.4 | all-reduce | flops 1 | bytes 8 | tf_op jit(solution)/shard_map/pmax | solution.py:140
  507.8 1.3 fusion.1
  (72 shorter events, 4.9 us)
Async XLA Ops:
  7.2 15.8 %copy-start.3 = (f32[2,256,512]{2,1,0:T(8,128)S(1)}, f32[2,256,512]{2,1,0:T(8,128)}, u32[]{:S(2)}) copy-start(f32[2,256,512]{2,1,0:T(8,128)} %param.15) | copy-start | bytes 3145732
  7.2 7.5 %copy-start.20 = (s32[1,1,4,2]{2,3,1,0:T(2,128)S(1)}, s32[1,1,4,2]{2,3,1,0:T(2,128)}, u32[]{:S(2)}) copy-start(s32[1,1,4,2]{2,3,1,0:T(2,128)} %param.18) | copy-start | bytes 100
  7.2 406.2 %all-reduce.2.cloned.1.call-start = ((), (), s32[]{:S(2)}) async-start(), calls=%async_computation | async-start | bytes 1572864 | tf_op jit(solution)/shard_map/psum | solution.py:139
  8.6 14.5 %collective-permute-start.1 = (f32[2,128,512]{2,1,0:T(8,128)S(1)}, f32[2,128,512]{2,1,0:T(8,128)S(1)}, u32[]{:S(2)}, u32[]{:S(2)}) collective-permute-start(f32[2,128,512]{2,1,0:T(8,128)S(1)} %get-tuple-element.183), channel_id=1, source_target_pairs={{32,0},{64,32},{96,64},{128,96},{160,128},{192,160},{224,192},{33,... | collective-permute-start | bytes 1572872 | tf_op jit(solution)/shard_map/ppermute | solution.py:17
  9.9 13.0 %collective-permute-start = (f32[2,128,512]{2,1,0:T(8,128)S(1)}, f32[2,128,512]{2,1,0:T(8,128)S(1)}, u32[]{:S(2)}, u32[]{:S(2)}) collective-permute-start(f32[2,128,512]{2,1,0:T(8,128)S(1)} %get-tuple-element.184), channel_id=1, source_target_pairs={{0,32},{32,64},{64,96},{96,128},{128,160},{160,192},{192,224},{1,3... | collective-permute-start | bytes 1572872 | tf_op jit(solution)/shard_map/ppermute | solution.py:15
  23.0 10.4 %copy-start.10 = (f32[2,256,256]{2,1,0:T(8,128)S(1)}, f32[2,256,256]{2,1,0:T(8,128)}, u32[]{:S(2)}) copy-start(f32[2,256,256]{2,1,0:T(8,128)} %param.16) | copy-start | bytes 1572868
  23.1 1.3 copy-start.6
  24.5 18.7 %collective-permute-start.2 = (f32[2,512,128]{2,1,0:T(8,128)S(1)}, f32[2,512,128]{2,1,0:T(8,128)S(1)}, u32[]{:S(2)}, u32[]{:S(2)}) collective-permute-start(f32[2,512,128]{2,1,0:T(8,128)S(1)} %get-tuple-element.181), channel_id=1, source_target_pairs={{0,1},{1,2},{2,3},{3,4},{4,5},{5,6},{6,7},{7,8},{8,9},{9,10},{10,1... | collective-permute-start | bytes 1572872 | tf_op jit(solution)/shard_map/ppermute | solution.py:15
  31.4 12.5 %collective-permute-start.3 = (f32[2,512,128]{2,1,0:T(8,128)S(1)}, f32[2,512,128]{2,1,0:T(8,128)}, u32[]{:S(2)}, u32[]{:S(2)}) collective-permute-start(f32[2,512,128]{2,1,0:T(8,128)S(1)} %get-tuple-element.182), channel_id=1, source_target_pairs={{1,0},{2,1},{3,2},{4,3},{5,4},{6,5},{7,6},{8,7},{9,8},{10,9},{11,1... | collective-permute-start | bytes 1572872 | tf_op jit(solution)/shard_map/ppermute | solution.py:17
  33.5 10.5 %copy-start.7 = (f32[2,512,512]{2,1,0:T(8,128)S(1)}, f32[2,512,512]{2,1,0:T(8,128)}, u32[]{:S(2)}) copy-start(f32[2,512,512]{2,1,0:T(8,128)} %copy-done.6) | copy-start | bytes 6291460
  43.1 0.8 copy-start.17
  56.7 1.9 copy-start.18
  56.7 1.9 copy-start.19
  62.3 1.2 copy-start.13
  67.8 1.6 copy-start.5
  67.8 1.6 copy-start.9
  69.4 1.6 copy-start.8
  136.7 10.1 %copy-start = (f32[3,512,768]{2,1,0:T(8,128)S(1)}, f32[3,512,768]{2,1,0:T(8,128)}, u32[]{:S(2)}) copy-start(f32[3,512,768]{2,1,0:T(8,128)} %get-tuple-element.129) | copy-start | bytes 14155780
  140.2 22.1 %collective-permute-start.4 = (f32[3,128,768]{2,1,0:T(8,128)}, f32[3,128,768]{2,1,0:T(8,128)}, u32[]{:S(2)}, u32[]{:S(2)}) collective-permute-start(f32[3,128,768]{2,1,0:T(8,128)} %get-tuple-element.170), channel_id=1, source_target_pairs={{0,32},{32,64},{64,96},{96,128},{128,160},{160,192},{192,224},{1,3... | collective-permute-start | bytes 3538952 | tf_op jit(solution)/shard_map/ppermute | solution.py:15
  145.4 1.6 copy-start.14
  145.4 1.6 copy-start.15
  145.4 1.6 copy-start.16
  145.4 22.1 %collective-permute-start.5 = (f32[3,128,768]{2,1,0:T(8,128)}, f32[3,128,768]{2,1,0:T(8,128)S(1)}, u32[]{:S(2)}, u32[]{:S(2)}) collective-permute-start(f32[3,128,768]{2,1,0:T(8,128)} %get-tuple-element.169), channel_id=1, source_target_pairs={{32,0},{64,32},{96,64},{128,96},{160,128},{192,160},{224,192},{33,... | collective-permute-start | bytes 3538952 | tf_op jit(solution)/shard_map/ppermute | solution.py:17
  167.8 253.0 %collective-permute-start.6 = (f32[3,256,128]{2,1,0:T(8,128)S(1)}, f32[3,256,128]{2,1,0:T(8,128)S(1)}, u32[]{:S(2)}, u32[]{:S(2)}) collective-permute-start(f32[3,256,128]{2,1,0:T(8,128)S(1)} %get-tuple-element.178), channel_id=1, source_target_pairs={{0,1},{1,2},{2,3},{3,4},{4,5},{5,6},{6,7},{7,8},{8,9},{9,10},{10,1... | collective-permute-start | bytes 1179656 | tf_op jit(solution)/shard_map/ppermute | solution.py:15
  415.7 10.6 %collective-permute-start.7 = (f32[3,256,128]{2,1,0:T(8,128)S(1)}, f32[3,256,128]{2,1,0:T(8,128)S(1)}, u32[]{:S(2)}, u32[]{:S(2)}) collective-permute-start(f32[3,256,128]{2,1,0:T(8,128)S(1)} %get-tuple-element.177), channel_id=1, source_target_pairs={{1,0},{2,1},{3,2},{4,3},{5,4},{6,5},{7,6},{8,7},{9,8},{10,9},{11,1... | collective-permute-start | bytes 1179656 | tf_op jit(solution)/shard_map/ppermute | solution.py:17
  420.8 7.5 %copy-start.11 = (f32[2,256,256]{2,1,0:T(8,128)S(1)}, f32[2,256,256]{2,1,0:T(8,128)}, u32[]{:S(2)}) copy-start(f32[2,256,256]{2,1,0:T(8,128)} %param.16) | copy-start | bytes 1572868
  420.9 7.5 %copy-start.12 = (f32[3,256,256]{2,1,0:T(8,128)S(1)}, f32[3,256,256]{2,1,0:T(8,128)}, u32[]{:S(2)}) copy-start(f32[3,256,256]{2,1,0:T(8,128)} %all-reduce.2.cloned.1.call-done) | copy-start | bytes 2359300
  420.9 86.9 %copy-start.4 = (f32[2,256,512]{2,1,0:T(8,128)S(1)}, f32[2,256,512]{2,1,0:T(8,128)}, u32[]{:S(2)}) copy-start(f32[2,256,512]{2,1,0:T(8,128)} %param.15) | copy-start | bytes 3145732
  426.4 1.2 copy-start.1
  428.3 79.4 %copy-start.2 = (f32[3,256,512]{2,1,0:T(8,128)S(1)}, f32[3,256,512]{2,1,0:T(8,128)}, u32[]{:S(2)}) copy-start(f32[3,256,512]{2,1,0:T(8,128)} %copy-done.1) | copy-start | bytes 4718596
Sparse Core Ops, SparseCore 0:
  148.1 265.2 all-reduce.1
where the time goes:
time: 518 us; the launch traced here: 516 us
  waiting for transfers between devices  270 us (52%)
  blocking collectives  77.9 us (15%)
  local copies, waits for them, and re-layouts  68.6 us (13%)
  starting transfers between devices  37.1 us (7%)
  other arithmetic  28 us (5%)
  between operations  16.4 us (3%)
  loops' own time  15.4 us (3%)
    psum x1, waiting for transfers between devices, body(): summed = lax.psum(probe_terms, ('row', 'col'))  234 us
    pmax x1, blocking collectives, body(): peak_illum = lax.pmax(jnp.max(illum), ('row', 'col'))  77.9 us
    dynamic_update_slice x4, local copies, waits for them, and re-layouts, add_one(): return lax.dynamic_update_slice(current, section, corner_at)  36.2 us
    ppermute x4, starting transfers between devices, extended(): lax.ppermute(tail, axis, [(i, (i + 1) % count) for i in range(ends)])  28.4 us
    ppermute x4, waiting for transfers between devices, extended(): lax.ppermute(tail, axis, [(i, (i + 1) % count) for i in range(ends)])  26.9 us
    another operation x1, loops' own time, place_terms(): return lax.fori_loop(0, term_set.shape[0], add_one, canvas)  15.4 us
    gather x12, local copies, waits for them, and re-layouts  11.3 us
  transfers between devices with their start and end apart: 9, of which 6 were waited for; matrix products, arithmetic and copies ran while one was open for 2% of the time, Pallas kernels for 0%

commit v1 on v0

v1 whole, which is shorter than its diff:
```python
import functools

import jax
import jax.numpy as jnp
import ml_dtypes
import numpy as np
from jax import lax
from jax.experimental import pallas as pl
from jax.experimental.pallas import tpu as pltpu
from jax.sharding import PartitionSpec as P

N = 256
HALF = 128
TH = 256
TW = 512
PAT = 4
CORES = 2
XS = 4
ZS = 8
YS = 4
CHUNK = 24
TILE = 8
DIRS = [(-1, 0), (1, 0), (0, -1), (0, 1), (-1, -1), (-1, 1), (1, -1), (1, 1)]
MESH = pl.DeviceIdType.MESH


def tables(extent):
    indices = np.arange(extent, dtype=np.int32)
    products = indices[:, None] * indices[None, :] % extent
    angles = 2.0 * np.pi / extent * products.astype(np.float64)
    cosine = np.cos(angles) / np.sqrt(float(extent))
    sine_part = np.sin(angles) / np.sqrt(float(extent))
    forward = np.block([[cosine, -sine_part], [sine_part, cosine]])
    inverse = np.block([[cosine, sine_part], [-sine_part, cosine]])
    return (
        forward.astype(np.float32).astype(ml_dtypes.bfloat16),
        inverse.astype(np.float32).astype(ml_dtypes.bfloat16),
    )


def span(step, size, middle):
    if step == 0:
        return pl.ds(HALF if middle else 0, size)
    if middle:
        return pl.ds(0 if step < 0 else size + HALF, HALF)
    return pl.ds(0 if step < 0 else size - HALF, HALF)


def landing(step, size):
    if step == 0:
        return pl.ds(HALF, size)
    return pl.ds(0 if step > 0 else size + HALF, HALF)


def kernel(
    pos,
    cnt,
    obj,
    probe_in,
    meas_in,
    fwd_in,
    inv_in,
    obj_out,
    probe_out,
    framed,
    probe,
    meas,
    meas_t,
    fwd,
    inv,
    padded,
    canvas,
    rx_v,
    rx_h,
    rx_c,
    patches,
    wave,
    exits,
    halves,
    residues,
    backs,
    s1,
    rx1,
    s2,
    rx2,
    s3,
    rx3,
    rx4,
    gathered,
    obj_new,
    probe_new,
    local_sem,
    halo_send,
    halo_recv,
    ill_send,
    ill_recv,
    grad_send,
    grad_recv,
    red_send,
    red_recv,
    out_sem,
):
    row = lax.axis_index("row")
    col = lax.axis_index("col")
    core = lax.rem(col, CORES)
    x_at = (row // YS) * 2 + lax.rem(col // 2, 2)
    z_at = col // 4
    y_at = lax.rem(row, YS)

    def core_peer():
        return (row, col + 1 - 2 * core)

    def x_peer(i):
        return ((i // 2) * YS + y_at, z_at * 4 + lax.rem(i, 2) * 2 + core)

    def z_peer(i):
        return (row, i * 4 + lax.rem(col, 4))

    def y_peer(i):
        return ((row // YS) * YS + i, col)

    def exists(step):
        near_row, near_col = row + step[0], col + step[1]
        conds = []
        if step[0] < 0:
            conds.append(near_row >= 0)
        if step[0] > 0:
            conds.append(near_row < lax.axis_size("row"))
        if step[1] < 0:
            conds.append(near_col >= 0)
        if step[1] > 0:
            conds.append(near_col < lax.axis_size("col"))
        return functools.reduce(jnp.logical_and, conds)

    center = (slice(None), pl.ds(HALF, TH), pl.ds(HALF, TW))
    local = [
        pltpu.make_async_copy(probe_in, probe, local_sem.at[0]),
        pltpu.make_async_copy(meas_in, meas, local_sem.at[1]),
        pltpu.make_async_copy(fwd_in, fwd, local_sem.at[2]),
        pltpu.make_async_copy(inv_in, inv, local_sem.at[3]),
        pltpu.make_async_copy(obj, framed.at[center], local_sem.at[4]),
    ]

    barrier = pltpu.get_barrier_semaphore()
    greeted = jnp.int32(0)
    for step in DIRS:
        there = exists(step)

        @pl.when(there)
        def _():
            pl.semaphore_signal(
                barrier, inc=1, device_id=(row + step[0], col + step[1]), device_id_type=MESH
            )

        greeted = greeted + there.astype(jnp.int32)
    pl.semaphore_signal(barrier, inc=1, device_id=core_peer(), device_id_type=MESH)
    for d in range(1, XS):
        pl.semaphore_signal(
            barrier, inc=1, device_id=x_peer(lax.rem(x_at + d, XS)), device_id_type=MESH
        )
    for d in range(1, ZS):
        pl.semaphore_signal(
            barrier, inc=1, device_id=z_peer(lax.rem(z_at + d, ZS)), device_id_type=MESH
        )
    for d in range(1, YS):
        pl.semaphore_signal(
            barrier, inc=1, device_id=y_peer(lax.rem(y_at + d, YS)), device_id_type=MESH
        )
    for copy in local:
        copy.start()
    pl.semaphore_wait(barrier, greeted + (CORES - 1 + XS - 1 + ZS - 1 + YS - 1))

    def halo_copy(n):
        dr, dc = DIRS[n]
        return pltpu.make_async_remote_copy(
            src_ref=obj.at[:, span(dr, TH, False), span(dc, TW, False)],
            dst_ref=framed.at[:, landing(dr, TH), landing(dc, TW)],
            send_sem=halo_send.at[n],
            recv_sem=halo_recv.at[n],
            device_id=(row + dr, col + dc),
            device_id_type=MESH,
        )

    def rx_of(n, planes):
        dr, dc = DIRS[n]
        if dc == 0:
            return rx_v.at[(dr + 1) // 2, planes]
        if dr == 0:
            return rx_h.at[(dc + 1) // 2, planes]
        return rx_c.at[(dr + 1) // 2, (dc + 1) // 2, planes]

    def term_copy(n, planes, send, recv):
        dr, dc = DIRS[n]
        return pltpu.make_async_remote_copy(
            src_ref=canvas.at[planes, span(dr, TH, True), span(dc, TW, True)],
            dst_ref=rx_of(n, planes),
            send_sem=send.at[n],
            recv_sem=recv.at[n],
            device_id=(row + dr, col + dc),
            device_id_type=MESH,
        )

    def ill_copy(n):
        return term_copy(n, pl.ds(2, 1), ill_send, ill_recv)

    def grad_copy(n):
        return term_copy(n, pl.ds(0, 2), grad_send, grad_recv)

    def for_each(make, order, act):
        for n in order:

            @pl.when(exists(DIRS[n]))
            def _():
                act(make(n))

    def opposite(n):
        return DIRS.index((-DIRS[n][0], -DIRS[n][1]))

    everywhere = range(len(DIRS))
    for_each(halo_copy, everywhere, lambda c: c.start())

    for n in everywhere:
        dr, dc = DIRS[n]
        opp = opposite(n)

        @pl.when(jnp.logical_not(exists(DIRS[n])))
        def _():
            rows, cols = landing(-dr, TH), landing(-dc, TW)
            framed[:, rows, cols] = jnp.zeros((2, rows.size, cols.size), jnp.float32)
            target = rx_of(opp, pl.ds(0, 3))
            target[...] = jnp.zeros(target.shape, jnp.float32)

    framed[:, TH + 2 * HALF :, :] = jnp.zeros((2, TILE, TW + 3 * HALF), jnp.float32)
    framed[:, : TH + 2 * HALF, TW + 2 * HALF :] = jnp.zeros(
        (2, TH + 2 * HALF, HALF), jnp.float32
    )

    def clear(i, carry):
        at = pl.ds(pl.multiple_of(i * 32, 32), 32)
        for k in range(PAT):
            for p in range(2):
                padded[k, p, at, :] = jnp.zeros((32, 640), jnp.float32)
        return carry

    lax.fori_loop(0, 24, clear, 0)

    count = cnt[0, 0]
    lives, tops, lefts, downs, overs = [], [], [], [], []
    for k in range(PAT):
        a = lax.max(lax.min(pos[k, 0] - (row * TH - HALF), TH), 0)
        b = lax.max(lax.min(pos[k, 1] - (col * TW - HALF), TW), 0)
        lives.append(jnp.where(k < count, 1.0, 0.0).astype(jnp.float32))
        tops.append(lax.div(a, TILE))
        downs.append(lax.rem(a, TILE))
        lefts.append(lax.div(b, 128))
        overs.append(lax.rem(b, 128))

    def lane_iota(shape):
        return lax.broadcasted_iota(jnp.int32, shape, len(shape) - 1)

    def sub_iota(shape):
        return lax.broadcasted_iota(jnp.int32, shape, len(shape) - 2)

    def window(p, k, first, tiles):
        s, r = downs[k], overs[k]
        rows = pl.ds((tops[k] + first) * TILE, (tiles + 1) * TILE)
        turned = []
        for j in range(3):
            cols = pl.ds((lefts[k] + j) * 128, 128)
            turned.append(pltpu.roll(framed[p, rows, cols], lax.rem(128 - r, 128), 1))
        near = lane_iota(turned[0].shape) < 128 - r
        found = []
        for j in range(2):
            both = jnp.where(near, turned[j], turned[j + 1]).reshape(tiles + 1, TILE, 128)
            both = pltpu.roll(both, lax.rem(TILE - s, TILE), 1)
            upper = sub_iota((tiles, TILE, 128)) < TILE - s
            found.append(
                jnp.where(upper, both[:tiles], both[1:]).reshape(tiles * TILE, 128)
            )
        return found

    def lay(k, p, tiles):
        s, r = downs[k], overs[k]
        moved = []
        for x in tiles:
            x = pltpu.roll(x.reshape(N // TILE, TILE, 128), s, 1)
            none = jnp.zeros((1, TILE, 128), jnp.float32)
            here = jnp.concatenate([x, none], axis=0)
            above = jnp.concatenate([none, x], axis=0)
            y = jnp.where(sub_iota(here.shape) >= s, here, above).reshape(N + TILE, 128)
            moved.append(pltpu.roll(y, r, 1))
        right = lane_iota((N + TILE, 128)) >= r
        rows = pl.ds(N, N + TILE)
        padded[k, p, rows, pl.ds(128, 128)] = jnp.where(right, moved[0], 0.0)
        padded[k, p, rows, pl.ds(256, 128)] = jnp.where(right, moved[1], moved[0])
        padded[k, p, rows, pl.ds(384, 128)] = jnp.where(right, 0.0, moved[1])

    def collect(start, stop, pairs):
        size = 8

        def one(i, carry):
            first = i * size
            rows = pl.ds(pl.multiple_of(first * TILE, size * TILE), size * TILE)
            for q, p in pairs:
                for j in range(6):
                    total = None
                    for k in range(PAT):
                        at = (first - tops[k] + N // TILE) * TILE
                        lane = lax.max(lax.min(j - lefts[k] + 1, 4), 0) * 128
                        part = padded[
                            k, p, pl.ds(at, size * TILE), pl.ds(lane, 128)
                        ]
                        total = part if total is None else total + part
                    canvas[q, rows, pl.ds(j * 128, 128)] = total
            return carry

        lax.fori_loop(start // size, stop // size, one, 0)

    local[0].wait()
    power = [
        probe[0, :, pl.ds(128 * j, 128)] * probe[0, :, pl.ds(128 * j, 128)]
        + probe[1, :, pl.ds(128 * j, 128)] * probe[1, :, pl.ds(128 * j, 128)]
        for j in range(2)
    ]
    for k in range(PAT):
        lay(k, 0, [lives[k] * x for x in power])
    collect(0, 64, [(2, 0)])
    local[1].wait()
    for k in range(PAT):
        meas_t[k] = meas[k].T
    for copy in local[2:]:
        copy.wait()

    for_each(halo_copy, everywhere, lambda c: c.wait_send())
    for n in everywhere:

        @pl.when(exists(DIRS[opposite(n)]))
        def _():
            halo_copy(n).wait_recv()

    for_each(ill_copy, everywhere, lambda c: c.start())

    def cut(i, carry):
        tiles = 4
        rows = pl.ds(pl.multiple_of(i * tiles * TILE, tiles * TILE), tiles * TILE)
        weight = [jnp.zeros((tiles * TILE, 128), jnp.float32)] * 2
        for k in range(PAT):
            real = window(0, k, i * tiles, tiles)
            imag = window(1, k, i * tiles, tiles)
            for j in range(2):
                cols = pl.ds(128 * j, 128)
                p_re, p_im = probe[0, rows, cols], probe[1, rows, cols]
                patches[k, 0, rows, cols] = real[j]
                patches[k, 1, rows, cols] = imag[j]
                exits[k, rows, cols] = (p_re * real[j] - p_im * imag[j]).astype(jnp.bfloat16)
                exits[k, rows, pl.ds(N + 128 * j, 128)] = (
                    p_re * imag[j] + p_im * real[j]
                ).astype(jnp.bfloat16)
                weight[j] = weight[j] + lives[k] * (real[j] * real[j] + imag[j] * imag[j])
        for j in range(2):
            s1[1, pl.ds(pl.multiple_of((1 + j) * N + i * tiles * TILE, 8), tiles * TILE), :] = (
                weight[j]
            )
        return carry

    lax.fori_loop(0, 8, cut, 0)

    def dot(a, b):
        return jnp.dot(a, b, preferred_element_type=jnp.float32)

    for k in range(PAT):
        half = dot(exits[k], fwd[...]).astype(jnp.bfloat16)
        halves[k, :N, :] = half[:, :N]
        halves[k, N:, :] = half[:, N:]
        spectrum = dot(inv[...], halves[k])
        re, im = spectrum[:N], spectrum[N:]
        factor = lives[k] * (1.0 - meas_t[k] * lax.rsqrt(re * re + im * im + 0.25))
        residues[k, :N, :] = (factor * re).astype(jnp.bfloat16)
        residues[k, N:, :] = (factor * im).astype(jnp.bfloat16)
        back = dot(fwd[...], residues[k]).astype(jnp.bfloat16)
        backs[k, :, :N] = back[:N]
        backs[k, :, N:] = back[N:]
        wave[k] = dot(backs[k], inv[...])

    def probe_sum(i, carry):
        size = 32
        at = pl.multiple_of(i * size, size)
        rows = pl.ds(at, size)
        for j in range(2):
            cols = pl.ds(128 * j, 128)
            real = imag = None
            for k in range(PAT):
                a, b = patches[k, 0, rows, cols], patches[k, 1, rows, cols]
                u, v = wave[k, rows, cols], wave[k, rows, pl.ds(N + 128 * j, 128)]
                one, two = a * u + b * v, a * v - b * u
                real = one if real is None else real + one
                imag = two if imag is None else imag + two
            s1[0, pl.ds(pl.multiple_of(j * N + at, 8), size), :] = real
            if j == 0:
                s1[0, pl.ds(pl.multiple_of(2 * N + at, 8), size), :] = imag
            else:
                s1[1, pl.ds(at, size), :] = imag
        return carry

    lax.fori_loop(0, N // 32, probe_sum, 0)

    for_each(ill_copy, everywhere, lambda c: c.wait_send())
    for n in everywhere:

        @pl.when(exists(DIRS[opposite(n)]))
        def _():
            ill_copy(n).wait_recv()

    def owned(p, rows, at, h, j):
        size = rows.size
        value = canvas[p, pl.ds(pl.multiple_of(HALF + h * HALF + at, 8), size), pl.ds(128 * (j + 1), 128)]
        near = pl.ds(at, size)
        value = value + rx_v[1 - h, p, near, pl.ds(128 * j, 128)]
        if j in (0, 3):
            side = 1 if j == 0 else 0
            value = value + rx_h[side, p, rows, :]
            value = value + rx_c[1 - h, side, p, near, :]
        return value

    size = 32
    peak = jnp.zeros((TILE, 128), jnp.float32)
    for h in range(2):

        def largest(i, most, h=h):
            at = pl.multiple_of(i * size, size)
            rows = pl.ds(pl.multiple_of(h * HALF + at, size), size)
            for j in range(4):
                value = owned(2, rows, at, h, j)
                canvas[2, pl.ds(pl.multiple_of(HALF + h * HALF + at, 8), size), pl.ds(128 * (j + 1), 128)] = value
                most = jnp.maximum(most, jnp.max(value.reshape(size // TILE, TILE, 128), axis=0))
            return most

        peak = lax.fori_loop(0, HALF // size, largest, peak)
    for c in range(CORES):
        s1[c, 3 * N :, :] = peak

    def send(src, dst, sem, peer):
        return pltpu.make_async_remote_copy(
            src_ref=src,
            dst_ref=dst,
            send_sem=red_send.at[sem],
            recv_sem=red_recv.at[sem],
            device_id=peer,
            device_id_type=MESH,
        )

    other = 1 - core
    first = send(s1.at[other], rx1, 0, core_peer())
    first.start()

    for k in range(PAT):
        parts = ([], [])
        for j in range(2):
            cols = pl.ds(128 * j, 128)
            u, v = wave[k, :, cols], wave[k, :, pl.ds(N + 128 * j, 128)]
            p_re, p_im = probe[0, :, cols], probe[1, :, cols]
            parts[0].append(p_re * u + p_im * v)
            parts[1].append(p_re * v - p_im * u)
        for p in range(2):
            lay(k, p, parts[p])

    both = [(0, 0), (1, 1)]
    collect(0, 16, both)
    for_each(grad_copy, [0, 4, 5], lambda c: c.start())
    collect(48, 64, both)
    for_each(grad_copy, [1, 6, 7], lambda c: c.start())
    collect(16, 48, both)
    for_each(grad_copy, [2, 3], lambda c: c.start())

    first.wait()
    part = 3 * N // XS
    for i in range(XS):
        at = pl.ds(i * part, part)
        s2[i, :part, :] = s1[core, at, :] + rx1[at, :]
    crown = jnp.maximum(s1[core, 3 * N :, :], rx1[3 * N :, :])
    for i in range(XS):
        s2[i, part:, :] = crown

    def x_copy(d):
        to = lax.rem(x_at + d, XS)
        return send(s2.at[to], rx2.at[d - 1], d, x_peer(to))

    for d in range(1, XS):
        x_copy(d).start()
    for d in range(1, XS):
        x_copy(d).wait()
    crown = s2[x_at, part:, :]
    for d in range(XS - 1):
        crown = jnp.maximum(crown, rx2[d, part:, :])
    for i in range(ZS):
        at = pl.ds(i * CHUNK, CHUNK)
        s3[i, :CHUNK, :] = (s2[x_at, at, :] + rx2[0, at, :]) + (rx2[1, at, :] + rx2[2, at, :])
        s3[i, CHUNK:, :] = crown

    def z_copy(d):
        to = lax.rem(z_at + d, ZS)
        return send(s3.at[to], rx3.at[d - 1], XS + d - 1, z_peer(to))

    for d in range(1, ZS):
        z_copy(d).start()
    for d in range(1, ZS):
        z_copy(d).wait()
    total = s3[z_at, :CHUNK, :]
    crown = s3[z_at, CHUNK:, :]
    for d in range(ZS - 1):
        total = total + rx3[d, :CHUNK, :]
        crown = jnp.maximum(crown, rx3[d, CHUNK:, :])
    rx4[y_at, :CHUNK, :] = total
    rx4[y_at, CHUNK:, :] = crown

    def y_copy(d):
        to = lax.rem(y_at + d, YS)
        return send(rx4.at[y_at], rx4.at[y_at], XS + ZS + d - 2, y_peer(to))

    for d in range(1, YS):
        y_copy(d).start()
    for d in range(1, YS):
        y_copy(d).wait()
    total = (rx4[0, :CHUNK, :] + rx4[1, :CHUNK, :]) + (rx4[2, :CHUNK, :] + rx4[3, :CHUNK, :])
    crown = jnp.maximum(
        jnp.maximum(rx4[0, CHUNK:, :], rx4[1, CHUNK:, :]),
        jnp.maximum(rx4[2, CHUNK:, :], rx4[3, CHUNK:, :]),
    )
    gathered[core, x_at, z_at] = total

    base = XS + ZS + YS - 2

    def z_back(d):
        to = lax.rem(z_at + d, ZS)
        mine = gathered.at[core, x_at, z_at]
        return send(mine, mine, base + d - 1, z_peer(to))

    def x_back(d):
        to = lax.rem(x_at + d, XS)
        mine = gathered.at[core, x_at]
        return send(mine, mine, base + ZS - 1 + d - 1, x_peer(to))

    for d in range(1, ZS):
        z_back(d).start()
    for d in range(1, ZS):
        z_back(d).wait()
    for d in range(1, XS):
        x_back(d).start()

    for_each(grad_copy, everywhere, lambda c: c.wait_send())
    for n in everywhere:

        @pl.when(exists(DIRS[opposite(n)]))
        def _():
            grad_copy(n).wait_recv()

    top = jnp.max(crown)
    for h in range(2):

        def renew(i, carry, h=h):
            at = pl.multiple_of(i * size, size)
            rows = pl.ds(pl.multiple_of(h * HALF + at, size), size)
            inner = pl.ds(pl.multiple_of(HALF + h * HALF + at, 8), size)
            for j in range(4):
                cols = pl.ds(128 * (j + 1), 128)
                share = 1.0 / (0.75 * canvas[2, inner, cols] + 0.25 * top)
                for p in range(2):
                    obj_new[p, rows, pl.ds(128 * j, 128)] = (
                        framed[p, inner, cols] - owned(p, rows, at, h, j) * share
                    )
            return carry

        lax.fori_loop(0, HALF // size, renew, 0)
    obj_store = pltpu.make_async_copy(obj_new, obj_out, out_sem.at[0])
    obj_store.start()

    for d in range(1, XS):
        x_back(d).wait()
    mine = gathered.at[core]
    last = send(mine, mine, base + ZS + XS - 2, core_peer())
    last.start()
    last.wait()

    flat = XS * ZS * CHUNK

    def sums(p, j):
        n = p * 2 + j
        steps = N // 8
        lines = []
        start = (n % 3) * N
        for c in range(start // CHUNK, -(-(start + N) // CHUNK)):
            lo = max(start, c * CHUNK) - c * CHUNK
            hi = min(start + N, (c + 1) * CHUNK) - c * CHUNK
            lines.append(gathered[n // 3, c // ZS, c % ZS, pl.ds(lo, hi - lo), :])
        return jnp.concatenate(lines, axis=0)

    weight = [sums(2, j) for j in range(2)]
    heavy = jnp.maximum(jnp.max(weight[0]), jnp.max(weight[1]))
    for j in range(2):
        cols = pl.ds(128 * j, 128)
        share = 1.0 / (0.75 * weight[j] + 0.25 * heavy)
        for p in range(2):
            probe_new[p, :, cols] = probe[p, :, cols] - sums(p, j) * share
    probe_store = pltpu.make_async_copy(probe_new, probe_out, out_sem.at[1])
    probe_store.start()
    probe_store.wait()
    obj_store.wait()


def body(object_field, probe, measured, positions, counts):
    forward, inverse = tables(N)
    any_space = pl.BlockSpec(memory_space=pl.ANY)
    smem = pl.BlockSpec(memory_space=pltpu.SMEM)
    f32 = jnp.float32
    bf16 = jnp.bfloat16
    red = 1 + (XS - 1) * 2 + (ZS - 1) * 2 + (YS - 1) + 1
    dma = pltpu.SemaphoreType.DMA
    return pl.pallas_call(
        kernel,
        out_shape=(
            jax.ShapeDtypeStruct((2, TH, TW), f32),
            jax.ShapeDtypeStruct((2, N, N), f32),
        ),
        in_specs=[smem, smem] + [any_space] * 5,
        out_specs=(any_space, any_space),
        scratch_shapes=[
            pltpu.VMEM((2, TH + 2 * HALF + TILE, TW + 3 * HALF), f32),
            pltpu.VMEM((2, N, N), f32),
            pltpu.VMEM((PAT, N, N), f32),
            pltpu.VMEM((PAT, N, N), f32),
            pltpu.VMEM((2 * N, 2 * N), bf16),
            pltpu.VMEM((2 * N, 2 * N), bf16),
            pltpu.VMEM((PAT, 2, 3 * N, 640), f32),
            pltpu.VMEM((3, TH + 2 * HALF, TW + 2 * HALF), f32),
            pltpu.VMEM((2, 3, HALF, TW), f32),
            pltpu.VMEM((2, 3, TH, HALF), f32),
            pltpu.VMEM((2, 2, 3, HALF, HALF), f32),
            pltpu.VMEM((PAT, 2, N, N), f32),
            pltpu.VMEM((PAT, N, 2 * N), f32),
            pltpu.VMEM((PAT, N, 2 * N), bf16),
            pltpu.VMEM((PAT, 2 * N, N), bf16),
            pltpu.VMEM((PAT, 2 * N, N), bf16),
            pltpu.VMEM((PAT, N, 2 * N), bf16),
            pltpu.VMEM((CORES, 3 * N + TILE, 128), f32),
            pltpu.VMEM((3 * N + TILE, 128), f32),
            pltpu.VMEM((XS, 3 * N // XS + TILE, 128), f32),
            pltpu.VMEM((XS - 1, 3 * N // XS + TILE, 128), f32),
            pltpu.VMEM((ZS, CHUNK + TILE, 128), f32),
            pltpu.VMEM((ZS - 1, CHUNK + TILE, 128), f32),
            pltpu.VMEM((YS, CHUNK + TILE, 128), f32),
            pltpu.VMEM((CORES, XS, ZS, CHUNK, 128), f32),
            pltpu.VMEM((2, TH, TW), f32),
            pltpu.VMEM((2, N, N), f32),
            dma((5,)),
            dma((8,)),
            dma((8,)),
            dma((8,)),
            dma((8,)),
            dma((8,)),
            dma((8,)),
            dma((red,)),
            dma((red,)),
            dma((2,)),
        ],
        compiler_params=pltpu.CompilerParams(
            collective_id=0, has_side_effects=True, vmem_limit_bytes=56 * 1024 * 1024
        ),
    )(
        positions.reshape(PAT, 2),
        counts,
        object_field,
        probe,
        measured.reshape(PAT, N, N),
        jnp.asarray(forward),
        jnp.asarray(inverse),
    )


def solution(mesh):
    in_specs = (
        P(None, "row", "col"),
        P(),
        P("row", "col", None, None, None),
        P("row", "col", None, None),
        P("row", "col"),
    )
    out_specs = (P(None, "row", "col"), P())
    return jax.shard_map(body, mesh=mesh, in_specs=in_specs, out_specs=out_specs, check_vma=False)
```

time: 518 us -> 107 us (0.21)
  waiting for transfers between devices: 270 us -> 0 us
  Pallas kernels: 0 us -> 101 us
  blocking collectives: 77.9 us -> 0 us
  local copies, waits for them, and re-layouts: 68.6 us -> 4.45 us
  starting transfers between devices: 37.1 us -> 0 us
  other arithmetic: 28 us -> 0 us
  loops' own time: 15.4 us -> 0 us
  between operations: 16.4 us -> 1.3 us
    psum x1 -> x0, waiting for transfers between devices: 234 us -> none  [body(): summed = lax.psum(probe_terms, ('row', 'col'))]
    pallas_call x0 -> x1, Pallas kernels: none -> 101 us  [body(): pl.pallas_call(kernel, out_shape=(jax.ShapeDtypeStruct((2, TH, TW), f32),...]
    pmax x1 -> x0, blocking collectives: 77.9 us -> none  [body(): peak_illum = lax.pmax(jnp.max(illum), ('row', 'col'))]
    ppermute x8 -> x0, starting transfers between devices: 37 us -> none  [the longest x4 28.4 us: extended(): lax.ppermute(tail, axis, [(i, (i + 1) % count) for i in range(ends)])]
    dynamic_update_slice x4 -> x0, local copies, waits for them, and re-layouts: 36.2 us -> none  [add_one(): return lax.dynamic_update_slice(current, section, corner_at)]
    ppermute x8 -> x0, waiting for transfers between devices: 35.7 us -> none  [the longest x4 26.9 us: extended(): lax.ppermute(tail, axis, [(i, (i + 1) % count) for i in range(ends)])]
    another operation x2 -> x0, loops' own time: 15.4 us -> none  [the longest x1 15.4 us: place_terms(): return lax.fori_loop(0, term_set.shape[0], add_one, canvas)]
    gather x12 -> x0, local copies, waits for them, and re-layouts: 11.3 us -> none
  transfers between devices with their start and end apart: 9 -> 0, of which waited for: 6 -> 0; matrix products, arithmetic and copies ran while one was open for 2% -> 0% of each run, Pallas kernels for 0% -> 0%
where the time goes in v1:
time: 107 us; the launch traced here: 106 us
  Pallas kernels  101 us (94%)
  local copies, waits for them, and re-layouts  4.45 us (4%)
  between operations  1.3 us (1%)
    pallas_call x1, Pallas kernels, body(): pl.pallas_call(kernel, out_shape=(jax.ShapeDtypeStruct((2, TH, TW), f32),...  101 us
    unnamed x6, local copies, waits for them, and re-layouts  3.79 us

profile of v1, /device:TPU:1, one launch (start us, length us, event | category | flops | bytes accessed | tf_op | source)
XLA Modules:
  0.0 106.4 jit_solution(15610208759683852013)
XLA Ops:
  1.3 0.0 copy-start.1
  1.3 0.7 copy-done.1
  2.0 0.7 copy.9.pos
  2.6 100.6 %shard_map.86 = (f32[2,256,512]{2,1,0:T(8,128)}, f32[2,256,256]{2,1,0:T(8,128)}) custom-call(s32[4,2]{1,0:T(4,128)} %copy.9.pos, s32[1,1]{1,0:T(1,128)S(6)} %copy.12.cnt, f32[2,256,512]{2,1,0:T(8,128)} %obj.1, f32[2,256,256]{2,1,0:T(8,128)} %probe_in.1, f32[4,256,256]{2,1,0:T(8,128)} %bitcast.2, bf16[512,512]{1,0:T(8,128)(2,1)} %constant.4.clone.fwd_in, ...), custom_call_target="tpu_custom_call" | custom-call | tf_op jit(solution)/shard_map/pallas_call | solution.py:618
  103.3 0.0 copy-start
  103.3 2.3 %copy.13 = f32[2,256,512]{2,1,0:T(8,128)} copy(f32[2,256,512]{2,1,0:T(8,128)} %get-tuple-element.4) | data formatting | bytes 2097152
  105.6 0.0 copy-done
  105.6 0.8 copy.14
Async XLA Ops:
  1.3 0.7 copy-start.1
  103.3 2.3 %copy-start = (f32[2,256,256]{2,1,0:T(8,128)S(1)}, f32[2,256,256]{2,1,0:T(8,128)}, u32[]{:S(2)}) copy-start(f32[2,256,256]{2,1,0:T(8,128)} %get-tuple-element.5) | copy-start | bytes 1572868

commit v2 on v1

v2 whole, which is shorter than its diff:
```python
import functools

import jax
import jax.numpy as jnp
import ml_dtypes
import numpy as np
from jax import lax
from jax.experimental import pallas as pl
from jax.experimental.pallas import tpu as pltpu
from jax.sharding import PartitionSpec as P

N = 256
HALF = 128
TH = 256
TW = 512
PAT = 4
CORES = 2
XS = 4
ZS = 8
YS = 4
GCHUNK = 16
CHUNK = 24
TILE = 8
DIRS = [(-1, 0), (1, 0), (0, -1), (0, 1), (-1, -1), (-1, 1), (1, -1), (1, 1)]
OWN = len(DIRS)
MESH = pl.DeviceIdType.MESH


def tables(extent):
    indices = np.arange(extent, dtype=np.int32)
    products = indices[:, None] * indices[None, :] % extent
    angles = 2.0 * np.pi / extent * products.astype(np.float64)
    cosine = np.cos(angles) / np.sqrt(float(extent))
    sine_part = np.sin(angles) / np.sqrt(float(extent))
    forward = np.block([[cosine, -sine_part], [sine_part, cosine]])
    inverse = np.block([[cosine, sine_part], [-sine_part, cosine]])
    return (
        forward.astype(np.float32).astype(ml_dtypes.bfloat16),
        inverse.astype(np.float32).astype(ml_dtypes.bfloat16),
    )


def edge(step, size):
    if step == 0:
        return pl.ds(0, size)
    return pl.ds(0 if step < 0 else size - HALF, HALF)


def margin(step, size):
    if step == 0:
        return pl.ds(HALF, size)
    return pl.ds(0 if step < 0 else size + HALF, HALF)


def kernel(
    pos_in,
    cnt_in,
    obj,
    probe_in,
    meas_in,
    fwd_in,
    inv_in,
    obj_new,
    probe_new,
    pos,
    cnt,
    framed,
    probe,
    power,
    ill,
    meas,
    meas_t,
    fwd,
    inv,
    padded,
    canvas,
    rx_v,
    rx_h,
    patches,
    wave,
    exits,
    halves,
    residues,
    backs,
    w1,
    rxw1,
    w2,
    rxw2,
    g1,
    rxg1,
    g2,
    rxg2,
    s3,
    rx3,
    rx4,
    gathered,
    local_sem,
    pos_send,
    pos_recv,
    cnt_send,
    cnt_recv,
    halo_send,
    halo_recv,
    grad_send,
    grad_recv,
    red_send,
    red_recv,
):
    row = lax.axis_index("row")
    col = lax.axis_index("col")
    core = lax.rem(col, CORES)
    x_at = (row // YS) * 2 + lax.rem(col // 2, 2)
    z_at = col // 4
    y_at = lax.rem(row, YS)

    def core_peer():
        return (row, col + 1 - 2 * core)

    def x_peer(i):
        return ((i // 2) * YS + y_at, z_at * 4 + lax.rem(i, 2) * 2 + core)

    def z_peer(i):
        return (row, i * 4 + lax.rem(col, 4))

    def y_peer(i):
        return ((row // YS) * YS + i, col)

    def exists(step):
        near_row, near_col = row + step[0], col + step[1]
        conds = []
        if step[0] < 0:
            conds.append(near_row >= 0)
        if step[0] > 0:
            conds.append(near_row < lax.axis_size("row"))
        if step[1] < 0:
            conds.append(near_col >= 0)
        if step[1] > 0:
            conds.append(near_col < lax.axis_size("col"))
        return functools.reduce(jnp.logical_and, conds)

    center = (slice(None), pl.ds(HALF, TH), pl.ds(HALF, TW))
    local = [
        pltpu.make_async_copy(probe_in, probe, local_sem.at[0]),
        pltpu.make_async_copy(meas_in, meas, local_sem.at[1]),
        pltpu.make_async_copy(fwd_in, fwd, local_sem.at[2]),
        pltpu.make_async_copy(inv_in, inv, local_sem.at[3]),
        pltpu.make_async_copy(obj, framed.at[center], local_sem.at[4]),
        pltpu.make_async_copy(pos_in, pos.at[OWN], local_sem.at[5]),
        pltpu.make_async_copy(cnt_in, cnt.at[OWN], local_sem.at[6]),
    ]

    def do_barrier():
        barrier = pltpu.get_barrier_semaphore()
        greeted = jnp.int32(0)
        for step in DIRS:
            there = exists(step)

            @pl.when(there)
            def _():
                pl.semaphore_signal(
                    barrier, inc=1, device_id=(row + step[0], col + step[1]), device_id_type=MESH
                )

            greeted = greeted + there.astype(jnp.int32)
        pl.semaphore_signal(barrier, inc=1, device_id=core_peer(), device_id_type=MESH)
        for d in range(1, XS):
            pl.semaphore_signal(
                barrier, inc=1, device_id=x_peer(lax.rem(x_at + d, XS)), device_id_type=MESH
            )
        for d in range(1, ZS):
            pl.semaphore_signal(
                barrier, inc=1, device_id=z_peer(lax.rem(z_at + d, ZS)), device_id_type=MESH
            )
        for d in range(1, YS):
            pl.semaphore_signal(
                barrier, inc=1, device_id=y_peer(lax.rem(y_at + d, YS)), device_id_type=MESH
            )
        for copy in local:
            copy.start()
        pl.semaphore_wait(barrier, greeted + (CORES - 1 + XS - 1 + ZS - 1 + YS - 1))

    def near(dr, dc):
        return (row + dr, col + dc)

    def remote(src, dst, send_sem, recv_sem, peer):
        return pltpu.make_async_remote_copy(
            src_ref=src,
            dst_ref=dst,
            send_sem=send_sem,
            recv_sem=recv_sem,
            device_id=peer,
            device_id_type=MESH,
        )

    def opposite(n):
        return DIRS.index((-DIRS[n][0], -DIRS[n][1]))

    def place_copy(n):
        return remote(pos_in, pos.at[opposite(n)], pos_send.at[n], pos_recv.at[n], near(*DIRS[n]))

    def count_copy(n):
        return remote(cnt_in, cnt.at[opposite(n)], cnt_send.at[n], cnt_recv.at[n], near(*DIRS[n]))

    strips = [pl.ds(0, HALF), pl.ds(TW - HALF, HALF), pl.ds(HALF, TW - 2 * HALF)]

    def shifted(cols):
        return pl.ds(cols.start + HALF, cols.size)

    def halo_v(n, part):
        dr = DIRS[n][0]
        sem = n * 3 + part
        return remote(
            obj.at[:, edge(dr, TH), strips[part]],
            framed.at[:, margin(-dr, TH), shifted(strips[part])],
            halo_send.at[sem],
            halo_recv.at[sem],
            near(dr, 0),
        )

    def halo_h(n):
        dc = DIRS[n][1]
        return remote(
            obj.at[:, :, edge(dc, TW)],
            framed.at[:, pl.ds(HALF, TH), margin(-dc, TW)],
            halo_send.at[4 + n],
            halo_recv.at[4 + n],
            near(0, dc),
        )

    def halo_c(n):
        dr, dc = DIRS[n]
        return remote(
            framed.at[:, margin(-dr, TH), shifted(edge(dc, TW))],
            framed.at[:, margin(-dr, TH), margin(-dc, TW)],
            halo_send.at[4 + n],
            halo_recv.at[4 + n],
            near(0, dc),
        )

    def grad_v(n, part):
        dr = DIRS[n][0]
        sem = n * 3 + part
        return remote(
            canvas.at[:, margin(dr, TH), shifted(strips[part])],
            rx_v.at[(dr + 1) // 2, :, :, strips[part]],
            grad_send.at[sem],
            grad_recv.at[sem],
            near(dr, 0),
        )

    def grad_h(n):
        dr, dc = DIRS[n]
        rows = margin(dr, TH)
        return remote(
            canvas.at[:, rows, margin(dc, TW)],
            rx_h.at[(dc + 1) // 2, :, rows],
            grad_send.at[4 + n],
            grad_recv.at[4 + n],
            near(0, dc),
        )

    vertical, level, diagonal = (0, 1), (2, 3), (4, 5, 6, 7)

    def start(make, order, *more):
        for n in order:

            @pl.when(exists(DIRS[n]))
            def _():
                make(n, *more).start()

    def arrive(make, order, *more):
        for n in order:

            @pl.when(exists(DIRS[n]))
            def _():
                make(n, *more).wait_send()

            @pl.when(exists(DIRS[opposite(n)]))
            def _():
                make(n, *more).wait_recv()

    def start_level(n):
        @pl.when(exists((0, DIRS[n][1])))
        def _():
            grad_h(n).start()

    def arrive_level(n):
        @pl.when(exists((0, DIRS[n][1])))
        def _():
            grad_h(n).wait_send()

        @pl.when(exists((0, -DIRS[n][1])))
        def _():
            grad_h(n).wait_recv()

    def do_place_send():
        start(place_copy, range(OWN))
        start(count_copy, range(OWN))

    def do_halo_send():
        start(halo_v, vertical, 0)
        start(halo_v, vertical, 1)
        start(halo_h, level)
        start(halo_v, vertical, 2)

    def do_halo_forward():
        arrive(halo_v, vertical, 0)
        arrive(halo_v, vertical, 1)
        for n in diagonal:
            @pl.when(exists((-DIRS[n][0], DIRS[n][1])))
            def _():
                halo_c(n).start()

    def do_halo_wait():
        arrive(halo_h, level)
        arrive(halo_v, vertical, 2)
        for n in diagonal:
            dr, dc = DIRS[n]

            @pl.when(exists((-dr, dc)))
            def _():
                halo_c(n).wait_send()

            @pl.when(exists((-dr, -dc)))
            def _():
                halo_c(n).wait_recv()

    def do_margins():
        for n in range(OWN):
            dr, dc = DIRS[n]

            @pl.when(jnp.logical_not(exists(DIRS[n])))
            def _():
                rows, cols = margin(dr, TH), margin(dc, TW)
                framed[:, rows, cols] = jnp.zeros((2, rows.size, cols.size), jnp.float32)
                cnt[n, 0, 0] = 0
                for k in range(PAT):
                    pos[n, 0, k] = 0
                    pos[n, 1, k] = 0

        for n in vertical:

            @pl.when(jnp.logical_not(exists(DIRS[n])))
            def _():
                rx_v[1 - n] = jnp.zeros((2, HALF, TW), jnp.float32)

        for n in level:

            @pl.when(jnp.logical_not(exists(DIRS[n])))
            def _():
                rx_h[3 - n] = jnp.zeros((2, TH + 2 * HALF, HALF), jnp.float32)

        framed[:, TH + 2 * HALF :, :] = jnp.zeros((2, TILE, TW + 3 * HALF), jnp.float32)
        framed[:, : TH + 2 * HALF, TW + 2 * HALF :] = jnp.zeros(
            (2, TH + 2 * HALF, HALF), jnp.float32
        )

    def clear(i, carry):
        at = pl.ds(pl.multiple_of(i * 32, 32), 32)
        for k in range(PAT):
            for p in range(2):
                padded[k, p, at, :] = jnp.zeros((32, 640), jnp.float32)
        return carry

    def do_clear():
        lax.fori_loop(0, 24, clear, 0)

    def do_probe_in():
        local[0].wait()

    def do_meas_in():
        for copy in local[1:5]:
            copy.wait()

    def do_place_in():
        for copy in local[5:]:
            copy.wait()
        arrive(place_copy, range(OWN))
        arrive(count_copy, range(OWN))

    lives, tops, lefts, downs, overs = [], [], [], [], []

    def do_places():
        for k in range(PAT):
            a = lax.max(lax.min(pos[OWN, 0, k] - (row * TH - HALF), TH), 0)
            b = lax.max(lax.min(pos[OWN, 1, k] - (col * TW - HALF), TW), 0)
            lives.append(jnp.where(k < cnt[OWN, 0, 0], 1.0, 0.0).astype(jnp.float32))
            tops.append(lax.div(a, TILE))
            downs.append(lax.rem(a, TILE))
            lefts.append(lax.div(b, 128))
            overs.append(lax.rem(b, 128))

    def lane_iota(shape):
        return lax.broadcasted_iota(jnp.int32, shape, len(shape) - 1)

    def sub_iota(shape):
        return lax.broadcasted_iota(jnp.int32, shape, len(shape) - 2)

    def window(p, k, first, tiles):
        s, r = downs[k], overs[k]
        rows = pl.ds((tops[k] + first) * TILE, (tiles + 1) * TILE)
        turned = []
        for j in range(3):
            cols = pl.ds((lefts[k] + j) * 128, 128)
            turned.append(pltpu.roll(framed[p, rows, cols], lax.rem(128 - r, 128), 1))
        near = lane_iota(turned[0].shape) < 128 - r
        found = []
        for j in range(2):
            both = jnp.where(near, turned[j], turned[j + 1]).reshape(tiles + 1, TILE, 128)
            both = pltpu.roll(both, lax.rem(TILE - s, TILE), 1)
            upper = sub_iota((tiles, TILE, 128)) < TILE - s
            found.append(
                jnp.where(upper, both[:tiles], both[1:]).reshape(tiles * TILE, 128)
            )
        return found

    def lay(k, p, tiles, s, r):
        moved = []
        for x in tiles:
            x = pltpu.roll(x.reshape(N // TILE, TILE, 128), s, 1)
            none = jnp.zeros((1, TILE, 128), jnp.float32)
            here = jnp.concatenate([x, none], axis=0)
            above = jnp.concatenate([none, x], axis=0)
            y = jnp.where(sub_iota(here.shape) >= s, here, above).reshape(N + TILE, 128)
            moved.append(pltpu.roll(y, r, 1))
        right = lane_iota((N + TILE, 128)) >= r
        rows = pl.ds(N, N + TILE)
        padded[k, p, rows, pl.ds(128, 128)] = jnp.where(right, moved[0], 0.0)
        padded[k, p, rows, pl.ds(256, 128)] = jnp.where(right, moved[1], moved[0])
        padded[k, p, rows, pl.ds(384, 128)] = jnp.where(right, 0.0, moved[1])

    def collect(start, stop, pairs):
        size = 8

        def one(i, carry):
            first = i * size
            rows = pl.ds(pl.multiple_of(first * TILE, size * TILE), size * TILE)
            for q, p in pairs:
                for j in range(6):
                    total = None
                    for k in range(PAT):
                        at = (first - tops[k] + N // TILE) * TILE
                        lane = lax.max(lax.min(j - lefts[k] + 1, 4), 0) * 128
                        part = padded[
                            k, p, pl.ds(at, size * TILE), pl.ds(lane, 128)
                        ]
                        total = part if total is None else total + part
                    canvas[q, rows, pl.ds(j * 128, 128)] = total
            return carry

        lax.fori_loop(start // size, stop // size, one, 0)

    def do_power():
        for j in range(2):
            cols = pl.ds(128 * j, 128)
            power[j] = probe[0, :, cols] * probe[0, :, cols] + probe[1, :, cols] * probe[1, :, cols]
        ill[...] = jnp.zeros((TH, TW), jnp.float32)

    def light(t, carry):
        high, left = [], []
        for k in range(PAT):
            alive = jnp.where(k < cnt[t, 0, 0], 1.0, 0.0).astype(jnp.float32)
            a = lax.max(lax.min(pos[t, 0, k] - row * TH, 384), -384) + 384
            b = lax.max(lax.min(pos[t, 1, k] - col * TW, 896), -640) + 640
            lay(k, 0, [alive * power[j] for j in range(2)], lax.rem(a, TILE), lax.rem(b, 128))
            high.append(lax.div(a, TILE) - 80)
            left.append(lax.div(b, 128) - 5)
        size = 8
        for i in range(0, TH // TILE, size):
            rows = pl.ds(i * TILE, size * TILE)
            for j in range(4):
                total = ill[rows, pl.ds(j * 128, 128)]
                for k in range(PAT):
                    at = lax.max(lax.min(i - high[k], 96 - size), 0) * TILE
                    lane = lax.max(lax.min(j - left[k] + 1, 4), 0) * 128
                    total = total + padded[k, 0, pl.ds(at, size * TILE), pl.ds(lane, 128)]
                ill[rows, pl.ds(j * 128, 128)] = total
        return carry

    def do_light():
        lax.fori_loop(0, len(DIRS) + 1, light, 0)

    def do_peak():
        def largest(i, most):
            rows = pl.ds(pl.multiple_of(i * 32, 32), 32)
            for j in range(4):
                value = ill[rows, pl.ds(128 * j, 128)]
                most = jnp.maximum(most, jnp.max(value.reshape(4, TILE, 128), axis=0))
            return most

        peak = lax.fori_loop(0, TH // 32, largest, jnp.zeros((TILE, 128), jnp.float32))
        for c in range(CORES):
            w1[c, N:, :] = peak

    def do_turn():
        for k in range(PAT):
            meas_t[k] = meas[k].T

    def cut(i, carry):
        tiles = 4
        rows = pl.ds(pl.multiple_of(i * tiles * TILE, tiles * TILE), tiles * TILE)
        weight = [jnp.zeros((tiles * TILE, 128), jnp.float32)] * 2
        for k in range(PAT):
            real = window(0, k, i * tiles, tiles)
            imag = window(1, k, i * tiles, tiles)
            for j in range(2):
                cols = pl.ds(128 * j, 128)
                p_re, p_im = probe[0, rows, cols], probe[1, rows, cols]
                patches[k, 0, rows, cols] = real[j]
                patches[k, 1, rows, cols] = imag[j]
                exits[k, rows, cols] = (p_re * real[j] - p_im * imag[j]).astype(jnp.bfloat16)
                exits[k, rows, pl.ds(N + 128 * j, 128)] = (
                    p_re * imag[j] + p_im * real[j]
                ).astype(jnp.bfloat16)
                weight[j] = weight[j] + lives[k] * (real[j] * real[j] + imag[j] * imag[j])
        for j in range(2):
            w1[j, rows, :] = weight[j]
        return carry

    def do_cut():
        lax.fori_loop(0, 8, cut, 0)

    def dot(a, b):
        return jnp.dot(a, b, preferred_element_type=jnp.float32)

    def do_transforms(first, last):
        for k in range(first, last):
            half = dot(exits[k], fwd[...]).astype(jnp.bfloat16)
            halves[k, :N, :] = half[:, :N]
            halves[k, N:, :] = half[:, N:]
            spectrum = dot(inv[...], halves[k])
            re, im = spectrum[:N], spectrum[N:]
            factor = lives[k] * (1.0 - meas_t[k] * lax.rsqrt(re * re + im * im + 0.25))
            residues[k, :N, :] = (factor * re).astype(jnp.bfloat16)
            residues[k, N:, :] = (factor * im).astype(jnp.bfloat16)
            back = dot(fwd[...], residues[k]).astype(jnp.bfloat16)
            backs[k, :, :N] = back[:N]
            backs[k, :, N:] = back[N:]
            wave[k] = dot(backs[k], inv[...])

    def probe_sum(i, carry):
        size = 32
        at = pl.multiple_of(i * size, size)
        rows = pl.ds(at, size)
        for j in range(2):
            cols = pl.ds(128 * j, 128)
            real = imag = None
            for k in range(PAT):
                a, b = patches[k, 0, rows, cols], patches[k, 1, rows, cols]
                u, v = wave[k, rows, cols], wave[k, rows, pl.ds(N + 128 * j, 128)]
                one, two = a * u + b * v, a * v - b * u
                real = one if real is None else real + one
                imag = two if imag is None else imag + two
            g1[j, rows, :] = real
            g1[j, pl.ds(pl.multiple_of(N + at, 8), size), :] = imag
        return carry

    def do_probe_sum():
        lax.fori_loop(0, N // 32, probe_sum, 0)

    def owned(p, rows, at, h, j):
        size = rows.size
        inner = pl.ds(pl.multiple_of(HALF + h * HALF + at, 8), size)
        value = canvas[p, inner, pl.ds(128 * (j + 1), 128)]
        value = value + rx_v[1 - h, p, pl.ds(at, size), pl.ds(128 * j, 128)]
        if j in (0, 3):
            value = value + rx_h[1 if j == 0 else 0, p, inner, :]
        return value

    size = 32

    def send(src, dst, sem, peer):
        return remote(src, dst, red_send.at[sem], red_recv.at[sem], peer)

    def w_core():
        return send(w1.at[1 - core], rxw1, 0, core_peer())

    def g_core():
        return send(g1.at[1 - core], rxg1, 1, core_peer())

    def w_x(d):
        to = lax.rem(x_at + d, XS)
        return send(w2.at[to], rxw2.at[d - 1], 1 + d, x_peer(to))

    def g_x(d):
        to = lax.rem(x_at + d, XS)
        return send(g2.at[to], rxg2.at[d - 1], 4 + d, x_peer(to))

    def z_copy(d):
        to = lax.rem(z_at + d, ZS)
        return send(s3.at[to], rx3.at[d - 1], 7 + d, z_peer(to))

    def y_copy(d):
        to = lax.rem(y_at + d, YS)
        return send(rx4.at[y_at], rx4.at[y_at], 14 + d, y_peer(to))

    def do_w_core_send():
        w_core().start()

    def do_w_core_sum():
        w_core().wait()
        part = N // XS
        crown = jnp.maximum(w1[core, N:, :], rxw1[N:, :])
        for i in range(XS):
            at = pl.ds(i * part, part)
            w2[i, :part, :] = w1[core, at, :] + rxw1[at, :]
            w2[i, part:, :] = crown

    def do_w_x_send():
        for d in range(1, XS):
            w_x(d).start()

    def do_w_x_sum():
        for d in range(1, XS):
            w_x(d).wait()
        part = N // XS
        crown = w2[x_at, part:, :]
        for d in range(XS - 1):
            crown = jnp.maximum(crown, rxw2[d, part:, :])
        size = CHUNK - GCHUNK
        for i in range(ZS):
            at = pl.ds(i * size, size)
            s3[i, GCHUNK:CHUNK, :] = (w2[x_at, at, :] + rxw2[0, at, :]) + (
                rxw2[1, at, :] + rxw2[2, at, :]
            )
            s3[i, CHUNK:, :] = crown

    def do_core_send():
        g_core().start()

    def do_core_sum():
        g_core().wait()
        part = 2 * N // XS
        for i in range(XS):
            at = pl.ds(i * part, part)
            g2[i] = g1[core, at, :] + rxg1[at, :]

    def do_x_send():
        for d in range(1, XS):
            g_x(d).start()

    def do_x_sum():
        for d in range(1, XS):
            g_x(d).wait()
        for i in range(ZS):
            at = pl.ds(i * GCHUNK, GCHUNK)
            s3[i, :GCHUNK, :] = (g2[x_at, at, :] + rxg2[0, at, :]) + (
                rxg2[1, at, :] + rxg2[2, at, :]
            )

    def do_z_send():
        for d in range(1, ZS):
            z_copy(d).start()

    def do_z_sum():
        for d in range(1, ZS):
            z_copy(d).wait()
        total = s3[z_at, :CHUNK, :]
        crown = s3[z_at, CHUNK:, :]
        for d in range(ZS - 1):
            total = total + rx3[d, :CHUNK, :]
            crown = jnp.maximum(crown, rx3[d, CHUNK:, :])
        rx4[y_at, :CHUNK, :] = total
        rx4[y_at, CHUNK:, :] = crown

    def do_y_send():
        for d in range(1, YS):
            y_copy(d).start()

    def do_y_sum():
        for d in range(1, YS):
            y_copy(d).wait()
        gathered[core, x_at, z_at] = (rx4[0, :CHUNK, :] + rx4[1, :CHUNK, :]) + (
            rx4[2, :CHUNK, :] + rx4[3, :CHUNK, :]
        )

    base = 18

    def z_back(d):
        to = lax.rem(z_at + d, ZS)
        mine = gathered.at[core, x_at, z_at]
        return send(mine, mine, base + d - 1, z_peer(to))

    def x_back(d):
        to = lax.rem(x_at + d, XS)
        mine = gathered.at[core, x_at]
        return send(mine, mine, base + ZS - 1 + d - 1, x_peer(to))

    def core_back():
        mine = gathered.at[core]
        return send(mine, mine, base + ZS + XS - 2, core_peer())

    def do_z_back():
        for d in range(1, ZS):
            z_back(d).start()

    def do_z_wait():
        for d in range(1, ZS):
            z_back(d).wait()

    def do_x_back():
        for d in range(1, XS):
            x_back(d).start()

    def do_x_wait():
        for d in range(1, XS):
            x_back(d).wait()

    def do_core_back():
        core_back().start()

    def do_core_wait():
        core_back().wait()

    def do_lay():
        for k in range(PAT):
            parts = ([], [])
            for j in range(2):
                cols = pl.ds(128 * j, 128)
                u, v = wave[k, :, cols], wave[k, :, pl.ds(N + 128 * j, 128)]
                p_re, p_im = probe[0, :, cols], probe[1, :, cols]
                parts[0].append(p_re * u + p_im * v)
                parts[1].append(p_re * v - p_im * u)
            for p in range(2):
                lay(k, p, parts[p], downs[k], overs[k])

    def do_collect(first, last):
        collect(first, last, [(0, 0), (1, 1)])

    def do_grad_send():
        for n in diagonal:
            start_level(n)
        start(grad_v, vertical, 2)
        for n in level:
            start_level(n)

    def do_grad_forward():
        for n in diagonal:
            arrive_level(n)
        for dr in (-1, 1):
            rows = margin(dr, TH)
            for dc in (-1, 1):
                cols = shifted(edge(dc, TW))
                canvas[:, rows, cols] = canvas[:, rows, cols] + rx_h[(1 - dc) // 2, :, rows, :]
        start(grad_v, vertical, 0)
        start(grad_v, vertical, 1)

    def do_grad_wait():
        for n in level:
            arrive_level(n)
        for part in range(3):
            arrive(grad_v, vertical, part)

    def do_object():
        crown = jnp.maximum(
            jnp.maximum(rx4[0, CHUNK:, :], rx4[1, CHUNK:, :]),
            jnp.maximum(rx4[2, CHUNK:, :], rx4[3, CHUNK:, :]),
        )
        top = jnp.max(crown)
        for h in range(2):

            def renew(i, carry, h=h):
                at = pl.multiple_of(i * size, size)
                rows = pl.ds(pl.multiple_of(h * HALF + at, size), size)
                inner = pl.ds(pl.multiple_of(HALF + h * HALF + at, 8), size)
                for j in range(4):
                    cols = pl.ds(128 * (j + 1), 128)
                    share = 1.0 / (0.75 * ill[rows, pl.ds(128 * j, 128)] + 0.25 * top)
                    for p in range(2):
                        obj_new[p, rows, pl.ds(128 * j, 128)] = (
                            framed[p, inner, cols] - owned(p, rows, at, h, j) * share
                        )
                return carry

            lax.fori_loop(0, HALF // size, renew, 0)

    def do_probe():
        weight = [gathered[j, :, :, GCHUNK:, :].reshape(N, 128) for j in range(2)]
        heavy = jnp.maximum(jnp.max(weight[0]), jnp.max(weight[1]))
        for j in range(2):
            cols = pl.ds(128 * j, 128)
            share = 1.0 / (0.75 * weight[j] + 0.25 * heavy)
            for p in range(2):
                total = gathered[j, 2 * p : 2 * p + 2, :, :GCHUNK, :].reshape(N, 128)
                probe_new[p, :, cols] = probe[p, :, cols] - total * share

    do_barrier()
    do_place_send()
    do_halo_send()
    do_margins()
    do_clear()
    do_probe_in()
    do_power()
    do_place_in()
    do_places()
    do_light()
    do_peak()
    do_halo_forward()
    do_meas_in()
    do_turn()
    do_halo_wait()
    do_cut()
    do_w_core_send()
    do_transforms(0, 2)
    do_w_core_sum()
    do_w_x_send()
    do_transforms(2, 4)
    do_probe_sum()
    do_core_send()
    do_lay()
    do_collect(0, 64)
    do_core_sum()
    do_x_send()
    do_grad_send()
    do_w_x_sum()
    do_x_sum()
    do_z_send()
    do_grad_forward()
    do_z_sum()
    do_y_send()
    do_y_sum()
    do_z_back()
    do_z_wait()
    do_x_back()
    do_grad_wait()
    do_object()
    do_x_wait()
    do_core_back()
    do_core_wait()
    do_probe()


def body(object_field, probe, measured, positions, counts):
    forward, inverse = tables(N)
    any_space = pl.BlockSpec(memory_space=pl.ANY)
    vmem = pl.BlockSpec(memory_space=pltpu.VMEM)
    f32 = jnp.float32
    bf16 = jnp.bfloat16
    red = 18 + (ZS - 1) + (XS - 1) + 1
    dma = pltpu.SemaphoreType.DMA
    return pl.pallas_call(
        kernel,
        out_shape=(pltpu.VMEM((2, TH, TW), f32), pltpu.VMEM((2, N, N), f32)),
        in_specs=[any_space] * 7,
        out_specs=(vmem, vmem),
        scratch_shapes=[
            pltpu.SMEM((OWN + 1, 2, PAT), jnp.int32),
            pltpu.SMEM((OWN + 1, 1, 1), jnp.int32),
            pltpu.VMEM((2, TH + 2 * HALF + TILE, TW + 3 * HALF), f32),
            pltpu.VMEM((2, N, N), f32),
            pltpu.VMEM((2, N, 128), f32),
            pltpu.VMEM((TH, TW), f32),
            pltpu.VMEM((PAT, N, N), f32),
            pltpu.VMEM((PAT, N, N), f32),
            pltpu.VMEM((2 * N, 2 * N), bf16),
            pltpu.VMEM((2 * N, 2 * N), bf16),
            pltpu.VMEM((PAT, 2, 3 * N, 640), f32),
            pltpu.VMEM((2, TH + 2 * HALF, TW + 2 * HALF), f32),
            pltpu.VMEM((2, 2, HALF, TW), f32),
            pltpu.VMEM((2, 2, TH + 2 * HALF, HALF), f32),
            pltpu.VMEM((PAT, 2, N, N), f32),
            pltpu.VMEM((PAT, N, 2 * N), f32),
            pltpu.VMEM((PAT, N, 2 * N), bf16),
            pltpu.VMEM((PAT, 2 * N, N), bf16),
            pltpu.VMEM((PAT, 2 * N, N), bf16),
            pltpu.VMEM((PAT, N, 2 * N), bf16),
            pltpu.VMEM((CORES, N + TILE, 128), f32),
            pltpu.VMEM((N + TILE, 128), f32),
            pltpu.VMEM((XS, N // XS + TILE, 128), f32),
            pltpu.VMEM((XS - 1, N // XS + TILE, 128), f32),
            pltpu.VMEM((CORES, 2 * N, 128), f32),
            pltpu.VMEM((2 * N, 128), f32),
            pltpu.VMEM((XS, 2 * N // XS, 128), f32),
            pltpu.VMEM((XS - 1, 2 * N // XS, 128), f32),
            pltpu.VMEM((ZS, CHUNK + TILE, 128), f32),
            pltpu.VMEM((ZS - 1, CHUNK + TILE, 128), f32),
            pltpu.VMEM((YS, CHUNK + TILE, 128), f32),
            pltpu.VMEM((CORES, XS, ZS, CHUNK, 128), f32),
            dma((7,)),
            dma((OWN,)),
            dma((OWN,)),
            dma((OWN,)),
            dma((OWN,)),
            dma((12,)),
            dma((12,)),
            dma((12,)),
            dma((12,)),
            dma((red,)),
            dma((red,)),
        ],
        compiler_params=pltpu.CompilerParams(
            collective_id=0, has_side_effects=True, vmem_limit_bytes=56 * 1024 * 1024
        ),
    )(
        positions.reshape(PAT, 2).T,
        counts,
        object_field,
        probe,
        measured.reshape(PAT, N, N),
        jnp.asarray(forward),
        jnp.asarray(inverse),
    )


def solution(mesh):
    in_specs = (
        P(None, "row", "col"),
        P(),
        P("row", "col", None, None, None),
        P("row", "col", None, None),
        P("row", "col"),
    )
    out_specs = (P(None, "row", "col"), P())
    return jax.shard_map(body, mesh=mesh, in_specs=in_specs, out_specs=out_specs, check_vma=False)
```

time: 107 us -> 83.2 us (0.78)
  Pallas kernels: 101 us -> 80 us
  local copies, waits for them, and re-layouts: 4.45 us -> 1.77 us
    pallas_call x1, Pallas kernels: 101 us -> 80 us  [body(): pl.pallas_call(kernel, out_shape=(pltpu.VMEM((2, TH, TW), f32), pltpu.VME...]
    unnamed x6 -> x2, local copies, waits for them, and re-layouts: 3.79 us -> 1.77 us
where the time goes in v2:
time: 83.2 us; the launch traced here: 83.1 us
  Pallas kernels  80 us (96%)
  local copies, waits for them, and re-layouts  1.77 us (2%)
  between operations  1.29 us (2%)
    pallas_call x1, Pallas kernels, body(): pl.pallas_call(kernel, out_shape=(pltpu.VMEM((2, TH, TW), f32), pltpu.VME...  80 us
    unnamed x2, local copies, waits for them, and re-layouts  1.77 us

profile of v2, /device:TPU:1, one launch (start us, length us, event | category | flops | bytes accessed | tf_op | source)
XLA Modules:
  0.0 83.1 jit_solution(11509883221877966999)
XLA Ops:
  1.3 80.0 %shard_map.86 = (f32[2,256,512]{2,1,0:T(8,128)S(1)}, f32[2,256,256]{2,1,0:T(8,128)S(1)}) custom-call(s32[2,4]{1,0:T(2,128)} %bitcast.5, s32[1,1]{1,0:T(1,128)S(6)} %copy.13.cnt_in, f32[2,256,512]{2,1,0:T(8,128)} %obj.1, f32[2,256,256]{2,1,0:T(8,128)} %probe_in.1, f32[4,256,256]{2,1,0:T(8,128)} %bitcast.4, bf16[512,512]{1,0:T(8,128)(2,1)} %constant.4.clone.fwd_in, ...), custom_call_target="tpu_custom_call" | custom-call | tf_op jit(solution)/shard_map/pallas_call | solution.py:841
  81.3 1.0 %copy.11 = f32[2,256,512]{2,1,0:T(8,128)} copy(f32[2,256,512]{2,1,0:T(8,128)S(1)} %get-tuple-element.2) | data formatting | bytes 2097152
  82.3 0.8 copy.12

commit v3 on v2

--- a/solution.py
+++ b/solution.py
@@ -23,6 +23,8 @@
 TILE = 8
 DIRS = [(-1, 0), (1, 0), (0, -1), (0, 1), (-1, -1), (-1, 1), (1, -1), (1, 1)]
 OWN = len(DIRS)
+NEAR = (1, 7, 2, 6, 3, 5, 4)
+FAR = NEAR[::-1] + (0,)
 MESH = pl.DeviceIdType.MESH
 
 
@@ -99,6 +101,10 @@
     pos_recv,
     cnt_send,
     cnt_recv,
+    halo_relay,
+    grad_relay,
+    halo_hop,
+    grad_hop,
     halo_send,
     halo_recv,
     grad_send,
@@ -175,6 +181,16 @@
             pl.semaphore_signal(
                 barrier, inc=1, device_id=y_peer(lax.rem(y_at + d, YS)), device_id_type=MESH
             )
+        for n in vertical:
+            near_end, relay_row, far_end = route(n)
+
+            @pl.when(row == far_end)
+            def _():
+                pl.semaphore_signal(
+                    barrier, inc=1, device_id=across(relay_row), device_id_type=MESH
+                )
+
+            greeted = greeted + (row == relay_row).astype(jnp.int32)
         for copy in local:
             copy.start()
         pl.semaphore_wait(barrier, greeted + (CORES - 1 + XS - 1 + ZS - 1 + YS - 1))
@@ -297,11 +313,88 @@
         start(place_copy, range(OWN))
         start(count_copy, range(OWN))
 
+    def route(n):
+        return (3, 7, 4) if DIRS[n][0] > 0 else (4, 0, 3)
+
+    def across(i):
+        return (i, col + 2 - 4 * lax.rem(col // 2, 2))
+
+    def leg_one(n, p, src, buf, sems):
+        return remote(src, buf.at[p], sems.at[p], sems.at[2 + p], across(route(n)[1]))
+
+    def leg_two(n, p, dst, buf, sems):
+        return remote(buf.at[p], dst, sems.at[4 + p], sems.at[6 + p], across(route(n)[2]))
+
+    def halo_ends(n, p):
+        dr = DIRS[n][0]
+        src = obj.at[p, edge(dr, TH), strips[2]]
+        return src, framed.at[p, margin(-dr, TH), shifted(strips[2])], halo_relay, halo_hop
+
+    def grad_ends(n, p):
+        dr = DIRS[n][0]
+        src = canvas.at[p, margin(dr, TH), shifted(strips[2])]
+        return src, rx_v.at[(dr + 1) // 2, p, :, strips[2]], grad_relay, grad_hop
+
+    def first_leg(n, p, ends):
+        src, dst, buf, sems = ends(n, p)
+        return leg_one(n, p, src, buf, sems)
+
+    def second_leg(n, p, ends):
+        src, dst, buf, sems = ends(n, p)
+        return leg_two(n, p, dst, buf, sems)
+
+    def start_middle(direct, ends):
+        for n in vertical:
+
+            @pl.when(row == route(n)[0])
+            def _():
+                for p in range(2):
+                    first_leg(n, p, ends).start()
+
+            @pl.when(exists(DIRS[n]) & (row != route(n)[0]))
+            def _():
+                direct(n, 2).start()
+
+    def relay_middle(ends):
+        for n in vertical:
+
+            @pl.when(row == route(n)[1])
+            def _():
+                for p in range(2):
+                    first_leg(n, p, ends).wait_recv()
+                    second_leg(n, p, ends).start()
+
+    def arrive_middle(direct, ends):
+        for n in vertical:
+
+            @pl.when(row == route(n)[0])
+            def _():
+                for p in range(2):
+                    first_leg(n, p, ends).wait_send()
+
+            @pl.when(exists(DIRS[n]) & (row != route(n)[0]))
+            def _():
+                direct(n, 2).wait_send()
+
+            @pl.when(row == route(n)[1])
+            def _():
+                for p in range(2):
+                    second_leg(n, p, ends).wait_send()
+
+            @pl.when(row == route(n)[2])
+            def _():
+                for p in range(2):
+                    second_leg(n, p, ends).wait_recv()
+
+            @pl.when(exists(DIRS[opposite(n)]) & (row != route(n)[2]))
+            def _():
+                direct(n, 2).wait_recv()
+
     def do_halo_send():
         start(halo_v, vertical, 0)
         start(halo_v, vertical, 1)
+        start_middle(halo_v, halo_ends)
         start(halo_h, level)
-        start(halo_v, vertical, 2)
 
     def do_halo_forward():
         arrive(halo_v, vertical, 0)
@@ -311,9 +404,12 @@
             def _():
                 halo_c(n).start()
 
+    def do_halo_relay():
+        relay_middle(halo_ends)
+
     def do_halo_wait():
         arrive(halo_h, level)
-        arrive(halo_v, vertical, 2)
+        arrive_middle(halo_v, halo_ends)
         for n in diagonal:
             dr, dc = DIRS[n]
 
@@ -538,25 +634,22 @@
             backs[k, :, N:] = back[N:]
             wave[k] = dot(backs[k], inv[...])
 
-    def probe_sum(i, carry):
+    def do_probe_sum():
         size = 32
-        at = pl.multiple_of(i * size, size)
-        rows = pl.ds(at, size)
-        for j in range(2):
-            cols = pl.ds(128 * j, 128)
-            real = imag = None
-            for k in range(PAT):
-                a, b = patches[k, 0, rows, cols], patches[k, 1, rows, cols]
-                u, v = wave[k, rows, cols], wave[k, rows, pl.ds(N + 128 * j, 128)]
-                one, two = a * u + b * v, a * v - b * u
-                real = one if real is None else real + one
-                imag = two if imag is None else imag + two
-            g1[j, rows, :] = real
-            g1[j, pl.ds(pl.multiple_of(N + at, 8), size), :] = imag
-        return carry
-
-    def do_probe_sum():
-        lax.fori_loop(0, N // 32, probe_sum, 0)
+        for i in range(N // size):
+            rows = pl.ds(i * size, size)
+            for j in range(2):
+                cols = pl.ds(128 * j, 128)
+                real = imag = None
+                for k in range(PAT):
+                    a, b = patches[k, 0, rows, cols], patches[k, 1, rows, cols]
+                    u, v = wave[k, rows, cols], wave[k, rows, pl.ds(N + 128 * j, 128)]
+                    one, two = a * u + b * v, a * v - b * u
+                    real = one if real is None else real + one
+                    imag = two if imag is None else imag + two
+                part = pl.ds((i % 2) * size, size)
+                g1[j, i // 2, part, :] = real
+                g1[j, ZS // 2 + i // 2, part, :] = imag
 
     def owned(p, rows, at, h, j):
         size = rows.size
@@ -572,27 +665,32 @@
     def send(src, dst, sem, peer):
         return remote(src, dst, red_send.at[sem], red_recv.at[sem], peer)
 
+    def ahead(d):
+        return lax.rem(z_at + d, ZS)
+
+    def behind(d):
+        return lax.rem(z_at + ZS - d, ZS)
+
     def w_core():
         return send(w1.at[1 - core], rxw1, 0, core_peer())
 
-    def g_core():
-        return send(g1.at[1 - core], rxg1, 1, core_peer())
-
-    def w_x(d):
-        to = lax.rem(x_at + d, XS)
-        return send(w2.at[to], rxw2.at[d - 1], 1 + d, x_peer(to))
-
-    def g_x(d):
-        to = lax.rem(x_at + d, XS)
-        return send(g2.at[to], rxg2.at[d - 1], 4 + d, x_peer(to))
+    def w_x(e):
+        to = lax.rem(x_at + e, XS)
+        return send(w2.at[to], rxw2.at[e - 1], e, x_peer(to))
+
+    def g_core(d):
+        return send(g1.at[1 - core, ahead(d)], rxg1.at[ahead(d)], 4 + d, core_peer())
+
+    def g_x(d, e):
+        to = lax.rem(x_at + e, XS)
+        return send(g2.at[ahead(d), to], rxg2.at[e - 1, ahead(d)], 11 + 3 * d + e, x_peer(to))
 
     def z_copy(d):
-        to = lax.rem(z_at + d, ZS)
-        return send(s3.at[to], rx3.at[d - 1], 7 + d, z_peer(to))
+        return send(s3.at[ahead(d)], rx3.at[d - 1], 35 + d, z_peer(ahead(d)))
 
     def y_copy(d):
         to = lax.rem(y_at + d, YS)
-        return send(rx4.at[y_at], rx4.at[y_at], 14 + d, y_peer(to))
+        return send(rx4.at[y_at], rx4.at[y_at], 42 + d, y_peer(to))
 
     def do_w_core_send():
         w_core().start()
@@ -601,9 +699,9 @@
         w_core().wait()
         part = N // XS
         crown = jnp.maximum(w1[core, N:, :], rxw1[N:, :])
+        total = (w1[core, :N, :] + rxw1[:N, :]).reshape(ZS, XS, TILE, 128)
         for i in range(XS):
-            at = pl.ds(i * part, part)
-            w2[i, :part, :] = w1[core, at, :] + rxw1[at, :]
+            w2[i, :part, :] = total[:, i].reshape(part, 128)
             w2[i, part:, :] = crown
 
     def do_w_x_send():
@@ -626,40 +724,33 @@
             s3[i, CHUNK:, :] = crown
 
     def do_core_send():
-        g_core().start()
+        for d in FAR:
+            g_core(d).start()
 
     def do_core_sum():
-        g_core().wait()
-        part = 2 * N // XS
-        for i in range(XS):
-            at = pl.ds(i * part, part)
-            g2[i] = g1[core, at, :] + rxg1[at, :]
-
-    def do_x_send():
-        for d in range(1, XS):
-            g_x(d).start()
+        for d in FAR:
+            g_core(d).wait()
+            at = ahead(d)
+            g2[at] = (g1[core, at] + rxg1[at]).reshape(XS, GCHUNK, 128)
+            for e in range(1, XS):
+                g_x(d, e).start()
 
     def do_x_sum():
-        for d in range(1, XS):
-            g_x(d).wait()
-        for i in range(ZS):
-            at = pl.ds(i * GCHUNK, GCHUNK)
-            s3[i, :GCHUNK, :] = (g2[x_at, at, :] + rxg2[0, at, :]) + (
-                rxg2[1, at, :] + rxg2[2, at, :]
-            )
-
-    def do_z_send():
-        for d in range(1, ZS):
-            z_copy(d).start()
+        for d in FAR:
+            for e in range(1, XS):
+                g_x(d, e).wait()
+            at = ahead(d)
+            s3[at, :GCHUNK, :] = (g2[at, x_at] + rxg2[0, at]) + (rxg2[1, at] + rxg2[2, at])
+            if d:
+                z_copy(d).start()
 
     def do_z_sum():
-        for d in range(1, ZS):
-            z_copy(d).wait()
         total = s3[z_at, :CHUNK, :]
         crown = s3[z_at, CHUNK:, :]
-        for d in range(ZS - 1):
-            total = total + rx3[d, :CHUNK, :]
-            crown = jnp.maximum(crown, rx3[d, CHUNK:, :])
+        for d in NEAR:
+            z_copy(d).wait()
+            total = total + rx3[d - 1, :CHUNK, :]
+            crown = jnp.maximum(crown, rx3[d - 1, CHUNK:, :])
         rx4[y_at, :CHUNK, :] = total
         rx4[y_at, CHUNK:, :] = crown
 
@@ -670,47 +761,43 @@
     def do_y_sum():
         for d in range(1, YS):
             y_copy(d).wait()
-        gathered[core, x_at, z_at] = (rx4[0, :CHUNK, :] + rx4[1, :CHUNK, :]) + (
+        gathered[core, z_at, x_at] = (rx4[0, :CHUNK, :] + rx4[1, :CHUNK, :]) + (
             rx4[2, :CHUNK, :] + rx4[3, :CHUNK, :]
         )
 
-    base = 18
-
     def z_back(d):
-        to = lax.rem(z_at + d, ZS)
-        mine = gathered.at[core, x_at, z_at]
-        return send(mine, mine, base + d - 1, z_peer(to))
-
-    def x_back(d):
-        to = lax.rem(x_at + d, XS)
-        mine = gathered.at[core, x_at]
-        return send(mine, mine, base + ZS - 1 + d - 1, x_peer(to))
-
-    def core_back():
-        mine = gathered.at[core]
-        return send(mine, mine, base + ZS + XS - 2, core_peer())
+        mine = gathered.at[core, z_at, x_at]
+        return send(mine, mine, 45 + d, z_peer(ahead(d)))
+
+    def x_back(d, e):
+        mine = gathered.at[core, behind(d), x_at]
+        return send(mine, mine, 52 + 3 * d + e, x_peer(lax.rem(x_at + e, XS)))
+
+    def core_back(d):
+        mine = gathered.at[core, behind(d)]
+        return send(mine, mine, 77 + d, core_peer())
 
     def do_z_back():
-        for d in range(1, ZS):
+        for d in NEAR[::-1]:
             z_back(d).start()
-
-    def do_z_wait():
-        for d in range(1, ZS):
+        for e in range(1, XS):
+            x_back(0, e).start()
+
+    def do_x_back():
+        for d in NEAR:
             z_back(d).wait()
-
-    def do_x_back():
-        for d in range(1, XS):
-            x_back(d).start()
-
-    def do_x_wait():
-        for d in range(1, XS):
-            x_back(d).wait()
+            for e in range(1, XS):
+                x_back(d, e).start()
 
     def do_core_back():
-        core_back().start()
+        for d in (0,) + NEAR:
+            for e in range(1, XS):
+                x_back(d, e).wait()
+            core_back(d).start()
 
     def do_core_wait():
-        core_back().wait()
+        for d in (0,) + NEAR:
+            core_back(d).wait()
 
     def do_lay():
         for k in range(PAT):
@@ -727,10 +814,17 @@
     def do_collect(first, last):
         collect(first, last, [(0, 0), (1, 1)])
 
-    def do_grad_send():
+    def do_grad_corner():
         for n in diagonal:
             start_level(n)
-        start(grad_v, vertical, 2)
+
+    def do_grad_middle():
+        start_middle(grad_v, grad_ends)
+
+    def do_grad_relay():
+        relay_middle(grad_ends)
+
+    def do_grad_level():
         for n in level:
             start_level(n)
 
@@ -748,8 +842,9 @@
     def do_grad_wait():
         for n in level:
             arrive_level(n)
-        for part in range(3):
+        for part in range(2):
             arrive(grad_v, vertical, part)
+        arrive_middle(grad_v, grad_ends)
 
     def do_object():
         crown = jnp.maximum(
@@ -781,7 +876,8 @@
             cols = pl.ds(128 * j, 128)
             share = 1.0 / (0.75 * weight[j] + 0.25 * heavy)
             for p in range(2):
-                total = gathered[j, 2 * p : 2 * p + 2, :, :GCHUNK, :].reshape(N, 128)
+                half = ZS // 2
+                total = gathered[j, half * p : half * (p + 1), :, :GCHUNK, :].reshape(N, 128)
                 probe_new[p, :, cols] = probe[p, :, cols] - total * share
 
     do_barrier()
@@ -798,6 +894,7 @@
     do_halo_forward()
     do_meas_in()
     do_turn()
+    do_halo_relay()
     do_halo_wait()
     do_cut()
     do_w_core_send()
@@ -808,24 +905,23 @@
     do_probe_sum()
     do_core_send()
     do_lay()
+    do_w_x_sum()
+    do_core_sum()
     do_collect(0, 64)
-    do_core_sum()
-    do_x_send()
-    do_grad_send()
-    do_w_x_sum()
+    do_grad_middle()
     do_x_sum()
-    do_z_send()
-    do_grad_forward()
+    do_grad_corner()
+    do_grad_level()
     do_z_sum()
     do_y_send()
+    do_grad_relay()
     do_y_sum()
     do_z_back()
-    do_z_wait()
+    do_grad_forward()
     do_x_back()
+    do_core_back()
     do_grad_wait()
     do_object()
-    do_x_wait()
-    do_core_back()
     do_core_wait()
     do_probe()
 
@@ -836,7 +932,7 @@
     vmem = pl.BlockSpec(memory_space=pltpu.VMEM)
     f32 = jnp.float32
     bf16 = jnp.bfloat16
-    red = 18 + (ZS - 1) + (XS - 1) + 1
+    red = 85
     dma = pltpu.SemaphoreType.DMA
     return pl.pallas_call(
         kernel,
@@ -868,19 +964,23 @@
             pltpu.VMEM((N + TILE, 128), f32),
             pltpu.VMEM((XS, N // XS + TILE, 128), f32),
             pltpu.VMEM((XS - 1, N // XS + TILE, 128), f32),
-            pltpu.VMEM((CORES, 2 * N, 128), f32),
-            pltpu.VMEM((2 * N, 128), f32),
-            pltpu.VMEM((XS, 2 * N // XS, 128), f32),
-            pltpu.VMEM((XS - 1, 2 * N // XS, 128), f32),
+            pltpu.VMEM((CORES, ZS, 2 * N // ZS, 128), f32),
+            pltpu.VMEM((ZS, 2 * N // ZS, 128), f32),
+            pltpu.VMEM((ZS, XS, GCHUNK, 128), f32),
+            pltpu.VMEM((XS - 1, ZS, GCHUNK, 128), f32),
             pltpu.VMEM((ZS, CHUNK + TILE, 128), f32),
             pltpu.VMEM((ZS - 1, CHUNK + TILE, 128), f32),
             pltpu.VMEM((YS, CHUNK + TILE, 128), f32),
-            pltpu.VMEM((CORES, XS, ZS, CHUNK, 128), f32),
+            pltpu.VMEM((CORES, ZS, XS, CHUNK, 128), f32),
             dma((7,)),
             dma((OWN,)),
             dma((OWN,)),
             dma((OWN,)),
             dma((OWN,)),
+            pltpu.VMEM((2, HALF, TW - 2 * HALF), f32),
+            pltpu.VMEM((2, HALF, TW - 2 * HALF), f32),
+            dma((8,)),
+            dma((8,)),
             dma((12,)),
             dma((12,)),
             dma((12,)),

time: 83.2 us -> 73.6 us (0.88)
  Pallas kernels: 80 us -> 70.4 us
    pallas_call x1, Pallas kernels: 80 us -> 70.4 us  [body(): pl.pallas_call(kernel, out_shape=(pltpu.VMEM((2, TH, TW), f32), pltpu.VME...]
where the time goes in v3:
time: 73.6 us; the launch traced here: 73.5 us
  Pallas kernels  70.4 us (96%)
  local copies, waits for them, and re-layouts  1.77 us (2%)
  between operations  1.29 us (2%)
    pallas_call x1, Pallas kernels, body(): pl.pallas_call(kernel, out_shape=(pltpu.VMEM((2, TH, TW), f32), pltpu.VME...  70.4 us
    unnamed x2, local copies, waits for them, and re-layouts  1.77 us

profile of v3, /device:TPU:1, one launch (start us, length us, event | category | flops | bytes accessed | tf_op | source)
XLA Modules:
  0.0 73.5 jit_solution(13190025501163766966)
XLA Ops:
  1.3 70.4 %shard_map.86 = (f32[2,256,512]{2,1,0:T(8,128)S(1)}, f32[2,256,256]{2,1,0:T(8,128)S(1)}) custom-call(s32[2,4]{1,0:T(2,128)} %bitcast.5, s32[1,1]{1,0:T(1,128)S(6)} %copy.13.cnt_in, f32[2,256,512]{2,1,0:T(8,128)} %obj.1, f32[2,256,256]{2,1,0:T(8,128)} %probe_in.1, f32[4,256,256]{2,1,0:T(8,128)} %bitcast.4, bf16[512,512]{1,0:T(8,128)(2,1)} %constant.4.clone.fwd_in, ...), custom_call_target="tpu_custom_call" | custom-call | tf_op jit(solution)/shard_map/pallas_call | solution.py:937
  71.7 1.0 %copy.11 = f32[2,256,512]{2,1,0:T(8,128)} copy(f32[2,256,512]{2,1,0:T(8,128)S(1)} %get-tuple-element.2) | data formatting | bytes 2097152
  72.7 0.8 %copy.12 = f32[2,256,256]{2,1,0:T(8,128)} copy(f32[2,256,256]{2,1,0:T(8,128)S(1)} %get-tuple-element.3) | data formatting | bytes 1048576

commit v4 on v3

--- a/solution.py
+++ b/solution.py
@@ -191,7 +191,7 @@
                 )
 
             greeted = greeted + (row == relay_row).astype(jnp.int32)
-        for copy in local:
+        for copy in local[:1] + local[5:]:
             copy.start()
         pl.semaphore_wait(barrier, greeted + (CORES - 1 + XS - 1 + ZS - 1 + YS - 1))
 
@@ -343,7 +343,7 @@
         src, dst, buf, sems = ends(n, p)
         return leg_two(n, p, dst, buf, sems)
 
-    def start_middle(direct, ends):
+    def start_legs(ends):
         for n in vertical:
 
             @pl.when(row == route(n)[0])
@@ -351,18 +351,20 @@
                 for p in range(2):
                     first_leg(n, p, ends).start()
 
+    def start_middle(direct):
+        for n in vertical:
+
             @pl.when(exists(DIRS[n]) & (row != route(n)[0]))
             def _():
                 direct(n, 2).start()
 
-    def relay_middle(ends):
+    def relay_middle(p, ends):
         for n in vertical:
 
             @pl.when(row == route(n)[1])
             def _():
-                for p in range(2):
-                    first_leg(n, p, ends).wait_recv()
-                    second_leg(n, p, ends).start()
+                first_leg(n, p, ends).wait_recv()
+                second_leg(n, p, ends).start()
 
     def arrive_middle(direct, ends):
         for n in vertical:
@@ -393,33 +395,83 @@
     def do_halo_send():
         start(halo_v, vertical, 0)
         start(halo_v, vertical, 1)
-        start_middle(halo_v, halo_ends)
+        for n in diagonal:
+
+            @pl.when(direct_from(n))
+            def _():
+                halo_d(n).start()
+
         start(halo_h, level)
+
+    def do_halo_middle():
+        start_legs(halo_ends)
+        start_middle(halo_v)
+
+    def halo_d(n):
+        dr, dc = DIRS[n]
+        return remote(
+            obj.at[:, edge(dr, TH), edge(dc, TW)],
+            framed.at[:, margin(-dr, TH), margin(-dc, TW)],
+            halo_send.at[8 + n],
+            halo_recv.at[8 + n],
+            near(dr, dc),
+        )
+
+    def leaves(dc):
+        return core == (1 if dc > 0 else 0)
+
+    def direct_from(n):
+        return (row == (2 if DIRS[n][0] > 0 else 5)) & exists((0, DIRS[n][1])) & leaves(DIRS[n][1])
+
+    def direct_to(n):
+        dr, dc = DIRS[n]
+        return (row == (3 if dr > 0 else 4)) & exists((0, -dc)) & leaves(-dc)
+
+    def handed_from(n):
+        dr, dc = DIRS[n]
+        apart = (row == (3 if dr > 0 else 4)) & leaves(dc)
+        return exists((-dr, dc)) & jnp.logical_not(apart)
+
+    def handed_to(n):
+        dr, dc = DIRS[n]
+        return exists((-dr, -dc)) & jnp.logical_not(direct_to(n))
 
     def do_halo_forward():
         arrive(halo_v, vertical, 0)
         arrive(halo_v, vertical, 1)
         for n in diagonal:
-            @pl.when(exists((-DIRS[n][0], DIRS[n][1])))
+
+            @pl.when(handed_from(n))
             def _():
                 halo_c(n).start()
 
-    def do_halo_relay():
-        relay_middle(halo_ends)
+    def do_halo_relay(p):
+        relay_middle(p, halo_ends)
 
     def do_halo_wait():
         arrive(halo_h, level)
         arrive_middle(halo_v, halo_ends)
         for n in diagonal:
-            dr, dc = DIRS[n]
-
-            @pl.when(exists((-dr, dc)))
+
+            @pl.when(handed_from(n))
             def _():
                 halo_c(n).wait_send()
 
-            @pl.when(exists((-dr, -dc)))
+            @pl.when(handed_to(n))
             def _():
                 halo_c(n).wait_recv()
+
+            @pl.when(direct_from(n))
+            def _():
+                halo_d(n).wait_send()
+
+            @pl.when(direct_to(n))
+            def _():
+                halo_d(n).wait_recv()
+
+    def do_local():
+        for copy in local[1:5]:
+            copy.start()
 
     def do_margins():
         for n in range(OWN):
@@ -674,51 +726,51 @@
     def w_core():
         return send(w1.at[1 - core], rxw1, 0, core_peer())
 
-    def w_x(e):
-        to = lax.rem(x_at + e, XS)
-        return send(w2.at[to], rxw2.at[e - 1], e, x_peer(to))
+    def w_y(e):
+        to = lax.rem(y_at + e, YS)
+        return send(w2.at[to], rxw2.at[e - 1], e, y_peer(to))
 
     def g_core(d):
         return send(g1.at[1 - core, ahead(d)], rxg1.at[ahead(d)], 4 + d, core_peer())
 
-    def g_x(d, e):
-        to = lax.rem(x_at + e, XS)
-        return send(g2.at[ahead(d), to], rxg2.at[e - 1, ahead(d)], 11 + 3 * d + e, x_peer(to))
+    def g_y(d, e):
+        to = lax.rem(y_at + e, YS)
+        return send(g2.at[ahead(d), to], rxg2.at[e - 1, ahead(d)], 11 + 3 * d + e, y_peer(to))
 
     def z_copy(d):
         return send(s3.at[ahead(d)], rx3.at[d - 1], 35 + d, z_peer(ahead(d)))
 
-    def y_copy(d):
-        to = lax.rem(y_at + d, YS)
-        return send(rx4.at[y_at], rx4.at[y_at], 42 + d, y_peer(to))
+    def x_copy(d):
+        to = lax.rem(x_at + d, XS)
+        return send(rx4.at[x_at], rx4.at[x_at], 42 + d, x_peer(to))
 
     def do_w_core_send():
         w_core().start()
 
     def do_w_core_sum():
         w_core().wait()
-        part = N // XS
+        part = N // YS
         crown = jnp.maximum(w1[core, N:, :], rxw1[N:, :])
-        total = (w1[core, :N, :] + rxw1[:N, :]).reshape(ZS, XS, TILE, 128)
-        for i in range(XS):
+        total = (w1[core, :N, :] + rxw1[:N, :]).reshape(ZS, YS, TILE, 128)
+        for i in range(YS):
             w2[i, :part, :] = total[:, i].reshape(part, 128)
             w2[i, part:, :] = crown
 
-    def do_w_x_send():
-        for d in range(1, XS):
-            w_x(d).start()
-
-    def do_w_x_sum():
-        for d in range(1, XS):
-            w_x(d).wait()
-        part = N // XS
-        crown = w2[x_at, part:, :]
-        for d in range(XS - 1):
+    def do_w_y_send():
+        for d in range(1, YS):
+            w_y(d).start()
+
+    def do_w_y_sum():
+        for d in range(1, YS):
+            w_y(d).wait()
+        part = N // YS
+        crown = w2[y_at, part:, :]
+        for d in range(YS - 1):
             crown = jnp.maximum(crown, rxw2[d, part:, :])
         size = CHUNK - GCHUNK
         for i in range(ZS):
             at = pl.ds(i * size, size)
-            s3[i, GCHUNK:CHUNK, :] = (w2[x_at, at, :] + rxw2[0, at, :]) + (
+            s3[i, GCHUNK:CHUNK, :] = (w2[y_at, at, :] + rxw2[0, at, :]) + (
                 rxw2[1, at, :] + rxw2[2, at, :]
             )
             s3[i, CHUNK:, :] = crown
@@ -731,16 +783,16 @@
         for d in FAR:
             g_core(d).wait()
             at = ahead(d)
-            g2[at] = (g1[core, at] + rxg1[at]).reshape(XS, GCHUNK, 128)
-            for e in range(1, XS):
-                g_x(d, e).start()
-
-    def do_x_sum():
+            g2[at] = (g1[core, at] + rxg1[at]).reshape(YS, GCHUNK, 128)
+            for e in range(1, YS):
+                g_y(d, e).start()
+
+    def do_y_sum():
         for d in FAR:
-            for e in range(1, XS):
-                g_x(d, e).wait()
+            for e in range(1, YS):
+                g_y(d, e).wait()
             at = ahead(d)
-            s3[at, :GCHUNK, :] = (g2[at, x_at] + rxg2[0, at]) + (rxg2[1, at] + rxg2[2, at])
+            s3[at, :GCHUNK, :] = (g2[at, y_at] + rxg2[0, at]) + (rxg2[1, at] + rxg2[2, at])
             if d:
                 z_copy(d).start()
 
@@ -751,27 +803,27 @@
             z_copy(d).wait()
             total = total + rx3[d - 1, :CHUNK, :]
             crown = jnp.maximum(crown, rx3[d - 1, CHUNK:, :])
-        rx4[y_at, :CHUNK, :] = total
-        rx4[y_at, CHUNK:, :] = crown
-
-    def do_y_send():
-        for d in range(1, YS):
-            y_copy(d).start()
-
-    def do_y_sum():
-        for d in range(1, YS):
-            y_copy(d).wait()
-        gathered[core, z_at, x_at] = (rx4[0, :CHUNK, :] + rx4[1, :CHUNK, :]) + (
+        rx4[x_at, :CHUNK, :] = total
+        rx4[x_at, CHUNK:, :] = crown
+
+    def do_x_send():
+        for d in range(1, XS):
+            x_copy(d).start()
+
+    def do_x_sum():
+        for d in range(1, XS):
+            x_copy(d).wait()
+        gathered[core, z_at, y_at] = (rx4[0, :CHUNK, :] + rx4[1, :CHUNK, :]) + (
             rx4[2, :CHUNK, :] + rx4[3, :CHUNK, :]
         )
 
     def z_back(d):
-        mine = gathered.at[core, z_at, x_at]
+        mine = gathered.at[core, z_at, y_at]
         return send(mine, mine, 45 + d, z_peer(ahead(d)))
 
-    def x_back(d, e):
-        mine = gathered.at[core, behind(d), x_at]
-        return send(mine, mine, 52 + 3 * d + e, x_peer(lax.rem(x_at + e, XS)))
+    def y_back(d, e):
+        mine = gathered.at[core, behind(d), y_at]
+        return send(mine, mine, 52 + 3 * d + e, y_peer(lax.rem(y_at + e, YS)))
 
     def core_back(d):
         mine = gathered.at[core, behind(d)]
@@ -780,19 +832,19 @@
     def do_z_back():
         for d in NEAR[::-1]:
             z_back(d).start()
-        for e in range(1, XS):
-            x_back(0, e).start()
-
-    def do_x_back():
+        for e in range(1, YS):
+            y_back(0, e).start()
+
+    def do_y_back():
         for d in NEAR:
             z_back(d).wait()
-            for e in range(1, XS):
-                x_back(d, e).start()
+            for e in range(1, YS):
+                y_back(d, e).start()
 
     def do_core_back():
         for d in (0,) + NEAR:
-            for e in range(1, XS):
-                x_back(d, e).wait()
+            for e in range(1, YS):
+                y_back(d, e).wait()
             core_back(d).start()
 
     def do_core_wait():
@@ -819,10 +871,13 @@
             start_level(n)
 
     def do_grad_middle():
-        start_middle(grad_v, grad_ends)
-
-    def do_grad_relay():
-        relay_middle(grad_ends)
+        start_middle(grad_v)
+
+    def do_grad_legs():
+        start_legs(grad_ends)
+
+    def do_grad_relay(p):
+        relay_middle(p, grad_ends)
 
     def do_grad_level():
         for n in level:
@@ -883,6 +938,8 @@
     do_barrier()
     do_place_send()
     do_halo_send()
+    do_halo_middle()
+    do_local()
     do_margins()
     do_clear()
     do_probe_in()
@@ -890,35 +947,38 @@
     do_place_in()
     do_places()
     do_light()
+    do_halo_forward()
     do_peak()
-    do_halo_forward()
     do_meas_in()
     do_turn()
-    do_halo_relay()
+    do_halo_relay(0)
+    do_halo_relay(1)
     do_halo_wait()
     do_cut()
     do_w_core_send()
     do_transforms(0, 2)
     do_w_core_sum()
-    do_w_x_send()
+    do_w_y_send()
     do_transforms(2, 4)
     do_probe_sum()
     do_core_send()
     do_lay()
-    do_w_x_sum()
+    do_w_y_sum()
     do_core_sum()
     do_collect(0, 64)
+    do_grad_legs()
     do_grad_middle()
+    do_grad_corner()
+    do_y_sum()
+    do_grad_relay(0)
+    do_z_sum()
+    do_x_send()
+    do_grad_relay(1)
+    do_grad_forward()
     do_x_sum()
-    do_grad_corner()
+    do_z_back()
     do_grad_level()
-    do_z_sum()
-    do_y_send()
-    do_grad_relay()
-    do_y_sum()
-    do_z_back()
-    do_grad_forward()
-    do_x_back()
+    do_y_back()
     do_core_back()
     do_grad_wait()
     do_object()
@@ -981,8 +1041,8 @@
             pltpu.VMEM((2, HALF, TW - 2 * HALF), f32),
             dma((8,)),
             dma((8,)),
-            dma((12,)),
-            dma((12,)),
+            dma((16,)),
+            dma((16,)),
             dma((12,)),
             dma((12,)),
             dma((red,)),

time: 73.6 us -> 69.9 us (0.950)
  Pallas kernels: 70.4 us -> 66.7 us
    pallas_call x1, Pallas kernels: 70.4 us -> 66.7 us  [body(): pl.pallas_call(kernel, out_shape=(pltpu.VMEM((2, TH, TW), f32), pltpu.VME...]
where the time goes in v4:
time: 69.9 us; the launch traced here: 69.8 us
  Pallas kernels  66.7 us (95%)
  local copies, waits for them, and re-layouts  1.77 us (3%)
  between operations  1.29 us (2%)
    pallas_call x1, Pallas kernels, body(): pl.pallas_call(kernel, out_shape=(pltpu.VMEM((2, TH, TW), f32), pltpu.VME...  66.7 us
    unnamed x2, local copies, waits for them, and re-layouts  1.77 us

profile of v4, /device:TPU:1, one launch (start us, length us, event | category | flops | bytes accessed | tf_op | source)
XLA Modules:
  0.0 69.8 jit_solution(6070848194617822660)
XLA Ops:
  1.3 66.7 %shard_map.86 = (f32[2,256,512]{2,1,0:T(8,128)S(1)}, f32[2,256,256]{2,1,0:T(8,128)S(1)}) custom-call(s32[2,4]{1,0:T(2,128)} %bitcast.5, s32[1,1]{1,0:T(1,128)S(6)} %copy.13.cnt_in, f32[2,256,512]{2,1,0:T(8,128)} %obj.1, f32[2,256,256]{2,1,0:T(8,128)} %probe_in.1, f32[4,256,256]{2,1,0:T(8,128)} %bitcast.4, bf16[512,512]{1,0:T(8,128)(2,1)} %constant.4.clone.fwd_in, ...), custom_call_target="tpu_custom_call" | custom-call | tf_op jit(solution)/shard_map/pallas_call | solution.py:997
  68.0 1.0 %copy.11 = f32[2,256,512]{2,1,0:T(8,128)} copy(f32[2,256,512]{2,1,0:T(8,128)S(1)} %get-tuple-element.2) | data formatting | bytes 2097152
  69.0 0.8 %copy.12 = f32[2,256,256]{2,1,0:T(8,128)} copy(f32[2,256,256]{2,1,0:T(8,128)S(1)} %get-tuple-element.3) | data formatting | bytes 1048576

commit v5 on v4

--- a/solution.py
+++ b/solution.py
@@ -596,7 +596,7 @@
                     canvas[q, rows, pl.ds(j * 128, 128)] = total
             return carry
 
-        lax.fori_loop(start // size, stop // size, one, 0)
+        lax.fori_loop(start // size, stop // size, one, 0, unroll=True)
 
     def do_power():
         for j in range(2):
@@ -666,25 +666,37 @@
         return carry
 
     def do_cut():
-        lax.fori_loop(0, 8, cut, 0)
+        lax.fori_loop(0, 8, cut, 0, unroll=True)
 
     def dot(a, b):
         return jnp.dot(a, b, preferred_element_type=jnp.float32)
 
     def do_transforms(first, last):
-        for k in range(first, last):
-            half = dot(exits[k], fwd[...]).astype(jnp.bfloat16)
-            halves[k, :N, :] = half[:, :N]
-            halves[k, N:, :] = half[:, N:]
-            spectrum = dot(inv[...], halves[k])
-            re, im = spectrum[:N], spectrum[N:]
-            factor = lives[k] * (1.0 - meas_t[k] * lax.rsqrt(re * re + im * im + 0.25))
-            residues[k, :N, :] = (factor * re).astype(jnp.bfloat16)
-            residues[k, N:, :] = (factor * im).astype(jnp.bfloat16)
-            back = dot(fwd[...], residues[k]).astype(jnp.bfloat16)
-            backs[k, :, :N] = back[:N]
-            backs[k, :, N:] = back[N:]
-            wave[k] = dot(backs[k], inv[...])
+        these = range(first, last)
+        for k in these:
+            for h in range(2):
+                rows = pl.ds(h * HALF, HALF)
+                half = dot(exits[k, rows, :], fwd[...]).astype(jnp.bfloat16)
+                halves[k, rows, :] = half[:, :N]
+                halves[k, pl.ds(N + h * HALF, HALF), :] = half[:, N:]
+        for k in these:
+            for h in range(2):
+                cols = pl.ds(h * HALF, HALF)
+                upper, lower = pl.ds(h * HALF, HALF), pl.ds(N + h * HALF, HALF)
+                re = dot(inv[upper, :], halves[k])
+                im = dot(inv[lower, :], halves[k])
+                factor = lives[k] * (1.0 - meas_t[k, upper, :] * lax.rsqrt(re * re + im * im + 0.25))
+                residues[k, upper, :] = (factor * re).astype(jnp.bfloat16)
+                residues[k, lower, :] = (factor * im).astype(jnp.bfloat16)
+        for k in these:
+            for h in range(2):
+                upper, lower = pl.ds(h * HALF, HALF), pl.ds(N + h * HALF, HALF)
+                backs[k, upper, :N] = dot(fwd[upper, :], residues[k]).astype(jnp.bfloat16)
+                backs[k, upper, N:] = dot(fwd[lower, :], residues[k]).astype(jnp.bfloat16)
+        for k in these:
+            for h in range(2):
+                rows = pl.ds(h * HALF, HALF)
+                wave[k, rows, :] = dot(backs[k, rows, :], inv[...])
 
     def do_probe_sum():
         size = 32
@@ -922,7 +934,7 @@
                         )
                 return carry
 
-            lax.fori_loop(0, HALF // size, renew, 0)
+            lax.fori_loop(0, HALF // size, renew, 0, unroll=True)
 
     def do_probe():
         weight = [gathered[j, :, :, GCHUNK:, :].reshape(N, 128) for j in range(2)]

time: 69.9 us -> 68.1 us (0.974)
  Pallas kernels: 66.7 us -> 65 us
    pallas_call x1, Pallas kernels: 66.7 us -> 65 us  [body(): pl.pallas_call(kernel, out_shape=(pltpu.VMEM((2, TH, TW), f32), pltpu.VME...]
where the time goes in v5:
time: 68.1 us; the launch traced here: 68 us
  Pallas kernels  65 us (95%)
  local copies, waits for them, and re-layouts  1.77 us (3%)
  between operations  1.29 us (2%)
    pallas_call x1, Pallas kernels, body(): pl.pallas_call(kernel, out_shape=(pltpu.VMEM((2, TH, TW), f32), pltpu.VME...  65 us
    unnamed x2, local copies, waits for them, and re-layouts  1.77 us

profile of v5, /device:TPU:1, one launch (start us, length us, event | category | flops | bytes accessed | tf_op | source)
XLA Modules:
  0.0 68.0 jit_solution(8635942895399517968)
XLA Ops:
  1.3 65.0 %shard_map.86 = (f32[2,256,512]{2,1,0:T(8,128)S(1)}, f32[2,256,256]{2,1,0:T(8,128)S(1)}) custom-call(s32[2,4]{1,0:T(2,128)} %bitcast.5, s32[1,1]{1,0:T(1,128)S(6)} %copy.13.cnt_in, f32[2,256,512]{2,1,0:T(8,128)} %obj.1, f32[2,256,256]{2,1,0:T(8,128)} %probe_in.1, f32[4,256,256]{2,1,0:T(8,128)} %bitcast.4, bf16[512,512]{1,0:T(8,128)(2,1)} %constant.4.clone.fwd_in, ...), custom_call_target="tpu_custom_call" | custom-call | tf_op jit(solution)/shard_map/pallas_call | solution.py:1009
  66.2 1.0 %copy.11 = f32[2,256,512]{2,1,0:T(8,128)} copy(f32[2,256,512]{2,1,0:T(8,128)S(1)} %get-tuple-element.2) | data formatting | bytes 2097152
  67.2 0.8 %copy.12 = f32[2,256,256]{2,1,0:T(8,128)} copy(f32[2,256,256]{2,1,0:T(8,128)S(1)} %get-tuple-element.3) | data formatting | bytes 1048576

commit v6 on v5

--- a/solution.py
+++ b/solution.py
@@ -343,13 +343,17 @@
         src, dst, buf, sems = ends(n, p)
         return leg_two(n, p, dst, buf, sems)
 
+    def whole(n, ends):
+        src, dst, buf, sems = ends(n, 1)
+        return remote(src, dst, sems.at[1], sems.at[3], near(DIRS[n][0], 0))
+
     def start_legs(ends):
         for n in vertical:
 
             @pl.when(row == route(n)[0])
             def _():
-                for p in range(2):
-                    first_leg(n, p, ends).start()
+                first_leg(n, 0, ends).start()
+                whole(n, ends).start()
 
     def start_middle(direct):
         for n in vertical:
@@ -371,8 +375,8 @@
 
             @pl.when(row == route(n)[0])
             def _():
-                for p in range(2):
-                    first_leg(n, p, ends).wait_send()
+                first_leg(n, 0, ends).wait_send()
+                whole(n, ends).wait_send()
 
             @pl.when(exists(DIRS[n]) & (row != route(n)[0]))
             def _():
@@ -380,13 +384,12 @@
 
             @pl.when(row == route(n)[1])
             def _():
-                for p in range(2):
-                    second_leg(n, p, ends).wait_send()
+                second_leg(n, 0, ends).wait_send()
 
             @pl.when(row == route(n)[2])
             def _():
-                for p in range(2):
-                    second_leg(n, p, ends).wait_recv()
+                second_leg(n, 0, ends).wait_recv()
+                whole(n, ends).wait_recv()
 
             @pl.when(exists(DIRS[opposite(n)]) & (row != route(n)[2]))
             def _():
@@ -960,11 +963,10 @@
     do_places()
     do_light()
     do_halo_forward()
+    do_halo_relay(0)
     do_peak()
     do_meas_in()
     do_turn()
-    do_halo_relay(0)
-    do_halo_relay(1)
     do_halo_wait()
     do_cut()
     do_w_core_send()
@@ -985,7 +987,6 @@
     do_grad_relay(0)
     do_z_sum()
     do_x_send()
-    do_grad_relay(1)
     do_grad_forward()
     do_x_sum()
     do_z_back()

time: 68.1 us -> 66.8 us (0.981)
  Pallas kernels: 65 us -> 63.9 us
    pallas_call x1, Pallas kernels: 65 us -> 63.9 us  [body(): pl.pallas_call(kernel, out_shape=(pltpu.VMEM((2, TH, TW), f32), pltpu.VME...]
where the time goes in v6:
time: 66.8 us; the launch traced here: 66.9 us
  Pallas kernels  63.9 us (96%)
  local copies, waits for them, and re-layouts  1.77 us (3%)
  between operations  1.29 us (2%)
    pallas_call x1, Pallas kernels, body(): pl.pallas_call(kernel, out_shape=(pltpu.VMEM((2, TH, TW), f32), pltpu.VME...  63.9 us
    unnamed x2, local copies, waits for them, and re-layouts  1.77 us

profile of v6, /device:TPU:1, one launch (start us, length us, event | category | flops | bytes accessed | tf_op | source)
XLA Modules:
  0.0 66.9 jit_solution(15162840440752630079)
XLA Ops:
  1.3 63.9 %shard_map.86 = (f32[2,256,512]{2,1,0:T(8,128)S(1)}, f32[2,256,256]{2,1,0:T(8,128)S(1)}) custom-call(s32[2,4]{1,0:T(2,128)} %bitcast.5, s32[1,1]{1,0:T(1,128)S(6)} %copy.13.cnt_in, f32[2,256,512]{2,1,0:T(8,128)} %obj.1, f32[2,256,256]{2,1,0:T(8,128)} %probe_in.1, f32[4,256,256]{2,1,0:T(8,128)} %bitcast.4, bf16[512,512]{1,0:T(8,128)(2,1)} %constant.4.clone.fwd_in, ...), custom_call_target="tpu_custom_call" | custom-call | tf_op jit(solution)/shard_map/pallas_call | solution.py:1010
  65.2 1.0 %copy.11 = f32[2,256,512]{2,1,0:T(8,128)} copy(f32[2,256,512]{2,1,0:T(8,128)S(1)} %get-tuple-element.2) | data formatting | bytes 2097152
  66.1 0.8 %copy.12 = f32[2,256,256]{2,1,0:T(8,128)} copy(f32[2,256,256]{2,1,0:T(8,128)S(1)} %get-tuple-element.3) | data formatting | bytes 1048576
